TPU v7x, 32 devices: a whole 2x2x4 slice. The times are simulated.
32 devices in a mesh: dp: 16 (over z, y, x), tensor: 2 (over core).
Axes of the slice: x: 2, y: 2, z: 4, core: 2. Of those that a mesh axis runs over, the one named last changes fastest.
Arguments:
- tokens: bfloat16 [2048, 768], P('dp'), may hold values from -6 to 6
- cotangent: bfloat16 [2048, 768], P('dp'), may hold values from -6 to 6
- seq_lengths: int32 [32], replicated, may hold values from 16 to 112, as said below
- seq_owner: int32 [32], replicated, may hold values from 0 to 15, as said below
- routes: int32 [2048, 1], P('dp'), may hold values from 0 to 3; in each aligned block of 128 rows (0 to 127, 128 to 255, ...) at most 42 rows name the same one
- rel_buckets: int32 [255], replicated, may hold values from 0 to 31
- attn_gain: float32 [768], replicated, may hold values from 0.5 to 1.5
- query_weight: bfloat16 [768, 768], P(None, 'tensor'), may hold values from -0.02734375 to 0.02734375
- key_weight: bfloat16 [768, 768], P(None, 'tensor'), may hold values from -0.21875 to 0.21875
- value_weight: bfloat16 [768, 768], P(None, 'tensor'), may hold values from -0.21875 to 0.21875
- output_weight: bfloat16 [768, 768], P('tensor'), may hold values from -1.75 to 1.75
- bias_table: float32 [32, 12], P(None, 'tensor'), may hold values from -4 to 4
- ffn_gain: float32 [768], replicated, may hold values from 0.5 to 1.5
- router_weight: bfloat16 [768, 4], replicated, may hold values from -0.15625 to 0.15625
- expert_in: bfloat16 [768, 12288], P(None, ('dp', 'tensor')), may hold values from -0.21875 to 0.21875
- expert_out: bfloat16 [12288, 768], P(('dp', 'tensor')), may hold values from -1.75 to 1.75
Outputs:
- output: bfloat16 [2048, 768], P('dp')
- tokens_grad: bfloat16 [2048, 768], P('dp')
- attn_gain_grad: float32 [768], replicated
- query_grad: float32 [768, 768], P(None, 'tensor')
- key_grad: float32 [768, 768], P(None, 'tensor')
- value_grad: float32 [768, 768], P(None, 'tensor')
- output_weight_grad: float32 [768, 768], P('tensor')
- table_grad: float32 [32, 12], P(None, 'tensor')
- ffn_gain_grad: float32 [768], replicated
- router_grad: float32 [768, 4], replicated
- expert_in_grad: float32 [768, 12288], P(None, ('dp', 'tensor'))
- expert_out_grad: float32 [12288, 768], P(('dp', 'tensor'))
Inputs may be any that keep to these rules, and one draw needn't show every extreme that they name: `seq_lengths`: each index of dp owns exactly two sequences, 2i and 2i + 1 for some i, whose lengths add up to 64 to 128; the two of some index add up to exactly 128. `seq_owner`: sequences 2i and 2i + 1 have the same owner, and every index of dp owns one such pair. `routes`: among the rows of one index of dp at most 42 name any one expert.
All inputs are finite; a program needn't handle non-finite values.
Results may differ from a plain program's by a relative error of at most 0.018.
Values may be sent and summed in bfloat16 or wider, within the bound.
A program may use at most 128 MiB of HBM per device.

v0:
```python
import jax
import jax.numpy as jnp
from jax import lax
from jax.sharding import PartitionSpec as P

HEAD_DIM = 64


epsilon = 1e-06


def rms_rows(rows, gain):
    scale = lax.rsqrt(jnp.mean(rows * rows, axis=-1, keepdims=True) + epsilon)
    return (rows * scale * gain, scale)


def rms_back(rows, gain, scale, grad):
    gain_grad = jnp.sum(grad * rows * scale, axis=0)
    inner = jnp.mean(rows * gain * grad, axis=-1, keepdims=True)
    return (scale * (gain * grad) - rows * (scale * scale * scale) * inner, gain_grad)


def block_layout(seq_lengths, seq_owner, rows):
    device = lax.axis_index("dp")
    mine = (seq_owner == device).astype(jnp.int32)
    owned = mine * seq_lengths
    starts = jnp.cumsum(owned) - owned
    slots = jnp.arange(rows, dtype=jnp.int32)
    inside = (
        (mine[:, None] > 0)
        & (slots[None, :] >= starts[:, None])
        & (slots[None, :] < (starts + owned)[:, None])
    ).astype(jnp.int32)
    count = jnp.sum(inside, axis=0)
    numbers = jnp.arange(seq_lengths.shape[0], dtype=jnp.int32)
    segment = jnp.sum(inside * numbers[:, None], axis=0)
    return (jnp.where(count > 0, segment, -1), count > 0)


def diagonal_sums(square):
    heads = square.shape[0]
    length = square.shape[1]
    flipped = square[:, ::-1, :]
    padded = jnp.pad(flipped, ((0, 0), (0, 0), (0, length)))
    flat = padded.reshape(heads, 2 * length * length)[:, : length * (2 * length - 1)]
    return jnp.sum(flat.reshape(heads, length, 2 * length - 1), axis=1)


def scores_of(queries, keys, bias, allowed):
    raw = jnp.einsum("ihc,jhc->hij", queries, keys, preferred_element_type=jnp.float32) + bias
    return jnp.where(allowed[None], raw, -1e30)


def send_out(rows_low, source, filled, experts, quarter, capacity):
    width = rows_low.shape[1]
    picked = jnp.where(filled[:, None], rows_low[source], jnp.zeros((), rows_low.dtype))
    copies = jnp.broadcast_to(
        picked.reshape(experts, 1, capacity, width), (experts, quarter, capacity, width)
    )
    arrived = lax.all_to_all(
        copies.reshape(experts * quarter, capacity, width),
        "dp",
        split_axis=0,
        concat_axis=0,
        tiled=True,
    )
    return arrived.reshape(experts * quarter * capacity, width)


def bring_back(part, slot, experts, quarter, capacity):
    width = part.shape[1]
    shaped = part.reshape(experts * quarter, capacity, width)
    returned = lax.all_to_all(
        shaped.astype(jnp.bfloat16), "dp", split_axis=0, concat_axis=0, tiled=True
    ).astype(shaped.dtype)
    table = jnp.sum(returned.reshape(experts, quarter, capacity, width), axis=1).reshape(
        experts * capacity, width
    )
    gathered = jnp.take(table, slot, axis=0, mode="fill", fill_value=0.0)
    return lax.psum(gathered.astype(jnp.bfloat16), "tensor").astype(jnp.float32)


def expert_forward(arrived, expert_in, expert_out):
    pre = jnp.dot(arrived, expert_in, preferred_element_type=jnp.float32)
    act_full, gelu_back = jax.vjp(jax.nn.gelu, pre)
    act = act_full.astype(jnp.bfloat16)
    part = jnp.dot(act, expert_out, preferred_element_type=jnp.float32)
    return (act, gelu_back, part)


def expert_backward(arrived_grad, gelu_back, expert_in, expert_out):
    act_grad = jnp.einsum("rd,fd->rf", arrived_grad, expert_out, preferred_element_type=jnp.float32)
    pre_grad = gelu_back(act_grad)[0].astype(jnp.bfloat16)
    input_part = jnp.einsum("rf,df->rd", pre_grad, expert_in, preferred_element_type=jnp.float32)
    return (pre_grad, input_part)


def local(
    tokens,
    cotangent,
    seq_lengths,
    seq_owner,
    routes,
    rel_buckets,
    attn_gain,
    query_weight,
    key_weight,
    value_weight,
    output_weight,
    bias_table,
    ffn_gain,
    router_weight,
    expert_in,
    expert_out,
):
    rows = tokens.shape[0]
    local_heads = query_weight.shape[1] // HEAD_DIM
    experts = router_weight.shape[1]
    groups = lax.axis_size("dp")
    quarter = groups // experts
    capacity = max(2, 4 * rows // (3 * experts))
    segment, valid = block_layout(seq_lengths, seq_owner, rows)
    keep = valid.astype(jnp.float32)
    inputs = tokens.astype(jnp.float32)
    normed_full, scale_one = rms_rows(inputs, attn_gain)
    normed = normed_full.astype(jnp.bfloat16)
    queries = (
        jnp.dot(normed, query_weight, preferred_element_type=jnp.float32)
        .astype(jnp.bfloat16)
        .reshape(rows, local_heads, HEAD_DIM)
    )
    keys = (
        jnp.dot(normed, key_weight, preferred_element_type=jnp.float32)
        .astype(jnp.bfloat16)
        .reshape(rows, local_heads, HEAD_DIM)
    )
    values = (
        jnp.dot(normed, value_weight, preferred_element_type=jnp.float32)
        .astype(jnp.bfloat16)
        .reshape(rows, local_heads, HEAD_DIM)
    )
    positions = jnp.arange(rows, dtype=jnp.int32)
    offsets = positions[None, :] - positions[:, None] + rows - 1
    lookup = (
        rel_buckets[:, None] == jnp.arange(bias_table.shape[0], dtype=jnp.int32)[None, :]
    ).astype(jnp.float32)
    relative = jnp.dot(lookup, bias_table, precision=lax.Precision.HIGHEST)
    bias = relative.T[:, offsets]
    allowed = (segment[:, None] == segment[None, :]) & valid[:, None] | (
        positions[:, None] == positions[None, :]
    )
    scores = scores_of(queries, keys, bias, allowed)
    top = jnp.max(scores, axis=-1, keepdims=True)
    weights = jnp.exp(scores - top)
    total = jnp.sum(weights, axis=-1, keepdims=True)
    probs = (weights / total).astype(jnp.bfloat16)
    log_total = top + jnp.log(total)
    mixed = (
        jnp.einsum("hij,jhc->ihc", probs, values, preferred_element_type=jnp.float32)
        .astype(jnp.bfloat16)
        .reshape(rows, -1)
    )
    attn_part = jnp.dot(mixed, output_weight, preferred_element_type=jnp.float32)
    attended = lax.psum(attn_part, "tensor") * keep[:, None]
    middle = inputs + attended
    normed_two_full, scale_two = rms_rows(middle, ffn_gain)
    normed_two = normed_two_full.astype(jnp.bfloat16)
    logits = jnp.dot(normed_two, router_weight, preferred_element_type=jnp.float32)
    gate_probs = jax.nn.softmax(logits, axis=-1)
    chosen = routes[:, 0]
    expert_ids = jnp.arange(experts, dtype=jnp.int32)
    route_hot = chosen[:, None] == expert_ids[None, :]
    gate = jnp.sum(gate_probs * route_hot.astype(jnp.float32), axis=-1)
    picked = (route_hot & valid[:, None]).astype(jnp.int32)
    rank = jnp.sum((jnp.cumsum(picked, axis=0) - picked) * picked, axis=1)
    slot = jnp.where(valid, chosen * capacity + rank, experts * capacity)
    places = jnp.arange(experts * capacity, dtype=jnp.int32)
    match = slot[None, :] == places[:, None]
    source = jnp.sum(match.astype(jnp.int32) * positions[None, :], axis=1)
    filled = jnp.any(match, axis=1)
    grad_out = cotangent.astype(jnp.float32)
    expert_grad = (gate[:, None] * grad_out).astype(jnp.bfloat16)
    arrived = send_out(normed_two, source, filled, experts, quarter, capacity)
    act, gelu_back, part = expert_forward(arrived, expert_in, expert_out)
    expert_rows = bring_back(part, slot, experts, quarter, capacity)
    arrived_grad = send_out(expert_grad, source, filled, experts, quarter, capacity)
    pre_grad, input_part = expert_backward(arrived_grad, gelu_back, expert_in, expert_out)
    expert_input_grad = bring_back(input_part, slot, experts, quarter, capacity)
    output = (middle + gate[:, None] * expert_rows).astype(jnp.bfloat16)
    gate_grad = jnp.sum(grad_out * expert_rows, axis=-1)
    logit_grad = (
        gate_probs * (route_hot.astype(jnp.float32) - gate[:, None]) * gate_grad[:, None]
    ).astype(jnp.bfloat16)
    router_grad = jnp.einsum(
        "td,te->de", normed_two, logit_grad, preferred_element_type=jnp.float32
    )
    expert_out_grad = jnp.einsum("rf,rd->fd", act, arrived_grad, preferred_element_type=jnp.float32)
    expert_in_grad = jnp.einsum("rd,rf->df", arrived, pre_grad, preferred_element_type=jnp.float32)
    normed_two_grad = expert_input_grad + jnp.einsum(
        "te,de->td", logit_grad, router_weight, preferred_element_type=jnp.float32
    )
    middle_part, ffn_gain_grad = rms_back(middle, ffn_gain, scale_two, normed_two_grad)
    middle_grad = grad_out + middle_part
    attn_grad = (middle_grad * keep[:, None]).astype(jnp.bfloat16)
    output_weight_grad = jnp.einsum(
        "tc,td->cd", mixed, attn_grad, preferred_element_type=jnp.float32
    )
    mixed_grad = (
        jnp.einsum("td,cd->tc", attn_grad, output_weight, preferred_element_type=jnp.float32)
        .astype(jnp.bfloat16)
        .reshape(rows, local_heads, HEAD_DIM)
    )
    scores_again = scores_of(queries, keys, bias, allowed)
    probs_full = jnp.exp(scores_again - log_total)
    probs_low = probs_full.astype(jnp.bfloat16)
    prob_grad = jnp.einsum("ihc,jhc->hij", mixed_grad, values, preferred_element_type=jnp.float32)
    values_grad = jnp.einsum(
        "hij,ihc->jhc", probs_low, mixed_grad, preferred_element_type=jnp.float32
    ).astype(jnp.bfloat16)
    score_grad = (
        probs_full * (prob_grad - jnp.sum(probs_full * prob_grad, axis=-1, keepdims=True))
    ).astype(jnp.bfloat16)
    queries_grad = (
        jnp.einsum("hij,jhc->ihc", score_grad, keys, preferred_element_type=jnp.float32)
        .astype(jnp.bfloat16)
        .reshape(rows, -1)
    )
    keys_grad = (
        jnp.einsum("hij,ihc->jhc", score_grad, queries, preferred_element_type=jnp.float32)
        .astype(jnp.bfloat16)
        .reshape(rows, -1)
    )
    values_grad = values_grad.reshape(rows, -1)
    table_grad = jnp.dot(
        lookup.T, diagonal_sums(score_grad.astype(jnp.float32)).T, precision=lax.Precision.HIGHEST
    )
    query_grad = jnp.einsum("td,tc->dc", normed, queries_grad, preferred_element_type=jnp.float32)
    key_grad = jnp.einsum("td,tc->dc", normed, keys_grad, preferred_element_type=jnp.float32)
    value_grad = jnp.einsum("td,tc->dc", normed, values_grad, preferred_element_type=jnp.float32)
    normed_part = (
        jnp.einsum("tc,dc->td", queries_grad, query_weight, preferred_element_type=jnp.float32)
        + jnp.einsum("tc,dc->td", keys_grad, key_weight, preferred_element_type=jnp.float32)
        + jnp.einsum("tc,dc->td", values_grad, value_weight, preferred_element_type=jnp.float32)
    )
    normed_grad = lax.psum(normed_part.astype(jnp.bfloat16), "tensor").astype(jnp.float32)
    input_part_grad, attn_gain_grad = rms_back(inputs, attn_gain, scale_one, normed_grad)
    tokens_grad = (middle_grad + input_part_grad).astype(jnp.bfloat16)
    summed = lax.psum(
        (
            attn_gain_grad,
            query_grad,
            key_grad,
            value_grad,
            output_weight_grad,
            table_grad,
            ffn_gain_grad,
            router_grad,
        ),
        "dp",
    )
    return (
        output,
        tokens_grad,
        summed[0],
        summed[1],
        summed[2],
        summed[3],
        summed[4],
        summed[5],
        summed[6],
        summed[7],
        expert_in_grad,
        expert_out_grad,
    )


def solution(mesh):
    return jax.shard_map(
        local,
        mesh=mesh,
        in_specs=(
            P("dp", None),
            P("dp", None),
            P(),
            P(),
            P("dp", None),
            P(),
            P(),
            P(None, "tensor"),
            P(None, "tensor"),
            P(None, "tensor"),
            P("tensor", None),
            P(None, "tensor"),
            P(),
            P(),
            P(None, ("dp", "tensor")),
            P(("dp", "tensor"), None),
        ),
        out_specs=(
            P("dp", None),
            P("dp", None),
            P(),
            P(None, "tensor"),
            P(None, "tensor"),
            P(None, "tensor"),
            P("tensor", None),
            P(None, "tensor"),
            P(),
            P(),
            P(None, ("dp", "tensor")),
            P(("dp", "tensor"), None),
        ),
        check_vma=False,
    )
```

profile of v0, /device:TPU:0, one launch (start us, length us, event | category | flops | bytes accessed | tf_op | source)
XLA Modules:
  0.0 502.6 jit_solution(9205262856042399901)
XLA Ops:
  7.3 0.8 fusion.41
  8.1 0.7 fusion.43
  8.8 1.1 fusion.18
  10.6 0.7 fusion.42
  11.4 1.5 convolution_convert_fusion.4
  14.5 54.5 %gather_fusion = f32[16384,6]{1,0:T(8,128)} fusion(f32[6,255]{0,1:T(8,128)S(1)} %copy.63, s32[16384]{0:T(1024)S(1)} %fusion.31), kind=kCustom, calls=%fused_computation.2 | custom fusion | bytes 851968 | tf_op jit(solution)/shard_map/gather | solution.py:148
  69.0 6.6 %copy.65 = f32[128,128,6]{0,1,2:T(8,128)S(1)} copy(f32[128,128,6]{2,1,0:T(8,128)} %bitcast.85) | data formatting | bytes 786432 | tf_op jit(solution)/shard_map/gather | solution.py:148
  77.1 1.0 fusion.60
  78.5 0.5 compare_and_fusion
  79.3 0.6 broadcast_in_dim.55
  79.9 19.6 %all-reduce.9.cloned.1.call-done = f32[128,768]{1,0:T(8,128)} async-done(((f32[128,768]{1,0:T(8,128)}), f32[128,768]{1,0:T(8,128)}) %all-reduce.9.cloned.1.call-update) | async-done | bytes 393232 | tf_op jit(solution)/shard_map/psum | solution.py:164
  99.5 1.2 multiply_reduce_fusion.3
  100.7 0.5 multiply_multiply_fusion.3
  101.2 0.6 copy-done.46
  102.1 0.6 select_reduce_fusion.3
  102.7 1.0 gather_fusion.1
  103.8 1.0 gather_fusion.2
  105.2 37.1 %all_to_all.20 = bf16[16,42,768]{2,1,0:T(8,128)(2,1)} all-to-all(bf16[16,42,768]{2,1,0:T(8,128)(2,1)S(1)} %bitcast.87), channel_id=1, replica_groups=mesh['dp'=16,'tensor'=2] {'dp'}, dimensions={0} | all-to-all | bytes 2064384 | tf_op jit(solution)/shard_map/all_to_all | solution.py:60
  142.3 1.1 broadcast_in_dim.61
  143.4 3.7 all-to-all-start
  147.1 2.2 reshape.332
  149.3 3.0 fusion.61
  152.4 20.7 %all-to-all-done = bf16[16,42,768]{2,1,0:T(8,128)(2,1)S(1)} async-done(((bf16[16,42,768]{2,1,0:T(8,128)(2,1)}), bf16[16,42,768]{2,1,0:T(8,128)(2,1)S(1)}, u32[]{:S(2)}, u32[]{:S(2)}) %all-to-all-start) | async-done | bytes 1032224 | tf_op jit(solution)/shard_map/all_to_all | solution.py:60
  173.1 1.1 reshape.327
  174.2 3.7 fusion.8
  177.9 1.0 copy-done.56
  178.9 0.8 convolution_convert_fusion.1
  179.7 1.2 convert_element_type.152
  180.9 6.1 %all-to-all-start.1 = ((bf16[16,42,768]{2,1,0:T(8,128)(2,1)}), bf16[16,42,768]{2,1,0:T(8,128)(2,1)S(1)}, u32[]{:S(2)}, u32[]{:S(2)}) async-start(bf16[16,42,768]{2,1,0:T(8,128)(2,1)} %convert_element_type.152), calls=%async_computation.1 | async-start | bytes 2359296 | tf_op jit(solution)/shard_map/all_to_all | solution.py:73
  187.0 2.7 convolution_convert_fusion
  189.7 2.2 convert_element_type.160
  191.9 20.8 %all-to-all-done.1 = bf16[16,42,768]{2,1,0:T(8,128)(2,1)S(1)} async-done(((bf16[16,42,768]{2,1,0:T(8,128)(2,1)}), bf16[16,42,768]{2,1,0:T(8,128)(2,1)S(1)}, u32[]{:S(2)}, u32[]{:S(2)}) %all-to-all-start.1) | async-done | bytes 1032224 | tf_op jit(solution)/shard_map/all_to_all | solution.py:73
  212.7 6.1 %all-to-all-start.3 = ((bf16[16,42,768]{2,1,0:T(8,128)(2,1)}), bf16[16,42,768]{2,1,0:T(8,128)(2,1)}, u32[]{:S(2)}, u32[]{:S(2)}) async-start(bf16[16,42,768]{2,1,0:T(8,128)(2,1)} %convert_element_type.160), calls=%async_computation.3 | async-start | bytes 2359296 | tf_op jit(solution)/shard_map/all_to_all | solution.py:73
  218.9 0.9 convert_reduce_fusion.1
  219.8 1.0 reshape.330
  220.8 23.8 %all-to-all-done.3 = bf16[16,42,768]{2,1,0:T(8,128)(2,1)} async-done(((bf16[16,42,768]{2,1,0:T(8,128)(2,1)}), bf16[16,42,768]{2,1,0:T(8,128)(2,1)}, u32[]{:S(2)}, u32[]{:S(2)}) %all-to-all-start.3) | async-done | bytes 1032224 | tf_op jit(solution)/shard_map/all_to_all | solution.py:73
  244.6 1.4 convert_reduce_fusion
  246.2 0.9 gather_fusion.3
  247.1 0.9 gather_fusion.4
  248.0 0.9 select_convert_fusion
  249.2 19.3 %all-reduce.15.cloned.1.call-done = (bf16[128,768]{1,0:T(8,128)(2,1)}, bf16[128,768]{1,0:T(8,128)(2,1)}) async-done(((bf16[128,768]{1,0:T(8,128)(2,1)}, bf16[128,768]{1,0:T(8,128)(2,1)}), (bf16[128,768]{1,0:T(8,128)(2,1)}, bf16[128,768]{1,0:T(8,128)(2,1)})) %all-reduce.15.cloned.1.call-update) | async-done | bytes 393232 | tf_op jit(solution)/shard_map/psum | solution.py:80
  268.5 1.1 fusion.12
  269.7 1.4 multiply_reduce_fusion
  271.1 1.5 convert_add_fusion.1
  274.6 1.4 fusion.45
  276.4 1.4 fusion.49
  278.2 1.4 fusion.47
  279.6 1.0 fusion.1
  280.7 1.4 fusion.51
  282.2 1.2 copy-done.14
  283.4 3.0 fusion.63
  286.4 1.8 fusion.46
  289.5 1.0 reshape.341
  291.0 9.1 %all-reduce.11.cloned.1.call-done = bf16[128,768]{1,0:T(8,128)(2,1)} async-done(((bf16[128,768]{1,0:T(8,128)(2,1)}), bf16[128,768]{1,0:T(8,128)(2,1)}) %all-reduce.11.cloned.1.call-update) | async-done | bytes 196624 | tf_op jit(solution)/shard_map/psum | solution.py:245
  300.1 1.1 fusion.23
  301.2 79.7 %all-reduce.1 = (f32[768]{0:T(1024)}, f32[32,6]{0,1:T(8,128)}, f32[768]{0:T(1024)}, f32[768,4]{0,1:T(4,128)}) all-reduce(f32[768]{0:T(1024)S(1)} %get-tuple-element.15, f32[32,6]{0,1:T(8,128)S(1)} %fusion.28, f32[768]{0:T(1024)S(1)} %get-tuple-element.13, f32[768,4]{0,1:T(4,128)S(1)} %fusion.59), channel_id=1, replica_groups=mesh['dp'=16,'tensor'=2] {'dp'}, use_global_device_ids=true, to_apply=%region_25.27 | all-reduce | flops 4800 | bytes 38400 | tf_op jit(solution)/shard_map/psum | solution.py:248
  380.9 1.8 fusion.16
  382.7 106.5 %all-reduce.13.cloned.1.call-done = (f32[768,384]{1,0:T(8,128)}, f32[768,384]{1,0:T(8,128)}, f32[768,384]{1,0:T(8,128)}, f32[384,768]{1,0:T(8,128)}) async-done(((f32[768,384]{1,0:T(8,128)}, f32[768,384]{1,0:T(8,128)}, f32[768,384]{1,0:T(8,128)}, f32[384,768]{1,0:T(8,128)}), (f32[768,384]{1,0:T(8,128)}, f32[768,384]{1,0:T(8,128)}, f32[768,384]{1,0:T(8,128)}, ...) | async-done | bytes 4718608 | tf_op jit(solution)/shard_map/psum | solution.py:248
  489.2 2.5 copy.90
  491.6 1.0 copy.91
  492.7 0.7 copy-done.12
  493.3 1.0 copy.92
  494.4 0.7 copy-done.11
  495.0 1.0 copy.93
  (178 shorter events, 10.1 us)
Async XLA Ops:
  7.2 167.0 %copy-start = (bf16[768,384]{1,0:T(8,128)(2,1)S(1)}, bf16[768,384]{1,0:T(8,128)(2,1)}, u32[]{:S(2)}) copy-start(bf16[768,384]{1,0:T(8,128)(2,1)} %param.32) | copy-start | bytes 1769476
  7.2 5.9 %copy-start.1 = (bf16[128,768]{1,0:T(8,128)(2,1)S(1)}, bf16[128,768]{1,0:T(8,128)(2,1)}, u32[]{:S(2)}) copy-start(bf16[128,768]{1,0:T(8,128)(2,1)} %param.18) | copy-start | bytes 589828
  7.2 5.9 %copy-start.25 = (f32[768]{0:T(1024)S(1)}, f32[768]{0:T(1024)}, u32[]{:S(2)}) copy-start(f32[768]{0:T(1024)} %param.24) | copy-start | bytes 9220
  7.2 5.9 %copy-start.7 = (bf16[768,384]{1,0:T(8,128)(2,1)S(1)}, bf16[768,384]{1,0:T(8,128)(2,1)}, u32[]{:S(2)}) copy-start(bf16[768,384]{1,0:T(8,128)(2,1)} %param.26) | copy-start | bytes 1769476
  7.2 92.2 %all-reduce.9.cloned.1.call-start = ((), (), s32[]{:S(2)}) async-start(), calls=%async_computation.4 | async-start | bytes 786432 | tf_op jit(solution)/shard_map/psum | solution.py:164
  8.8 4.8 copy-start.3
  10.4 3.6 copy-start.27
  12.9 1.1 copy-start.53
  12.9 1.1 copy-start.54
  13.1 62.6 %copy-start.15 = (bf16[128,384]{0,1:T(8,128)(2,1)}, bf16[128,384]{0,1:T(8,128)(2,1)S(1)}, u32[]{:S(2)}) copy-start(bf16[128,384]{0,1:T(8,128)(2,1)S(1)} %copy.61) | copy-start | bytes 294916
  13.6 62.1 %copy-start.17 = (bf16[128,384]{0,1:T(8,128)(2,1)}, bf16[128,384]{0,1:T(8,128)(2,1)S(1)}, u32[]{:S(2)}) copy-start(bf16[128,384]{0,1:T(8,128)(2,1)S(1)} %copy.62) | copy-start | bytes 294916
  14.1 62.0 %copy-start.23 = (bf16[128,384]{0,1:T(8,128)(2,1)}, bf16[128,384]{0,1:T(8,128)(2,1)S(1)}, u32[]{:S(2)}) copy-start(bf16[128,384]{0,1:T(8,128)(2,1)S(1)} %copy.59) | copy-start | bytes 294916
  76.0 1.1 copy-start.4
  76.1 0.6 copy-start.36
  76.1 2.0 copy-start.31
  76.7 24.0 %copy-start.21 = (bf16[6,64,128]{2,1,0:T(8,128)(2,1)}, bf16[6,64,128]{2,1,0:T(8,128)(2,1)S(1)}, u32[]{:S(2)}) copy-start(bf16[6,64,128]{2,1,0:T(8,128)(2,1)S(1)} %convolution_convert_fusion.9) | copy-start | bytes 294916
  77.1 24.7 %copy-start.26 = (f32[768]{0:T(1024)S(1)}, f32[768]{0:T(1024)}, u32[]{:S(2)}) copy-start(f32[768]{0:T(1024)} %param.30) | copy-start | bytes 9220
  78.1 23.8 %copy-start.29 = (bf16[768,4]{0,1:T(4,128)(2,1)S(1)}, bf16[768,4]{0,1:T(4,128)(2,1)}, u32[]{:S(2)}) copy-start(bf16[768,4]{0,1:T(4,128)(2,1)} %param.31) | copy-start | bytes 18436
  79.1 0.8 copy-start.51
  79.1 22.1 %copy-start.41 = (f32[128]{0:T(128)}, f32[128]{0:T(128)S(1)}, u32[]{:S(2)}) copy-start(f32[128]{0:T(128)S(1)} %get-tuple-element.45) | copy-start | bytes 1540
  102.0 1.7 copy-start.9
  102.7 1.0 copy-start.38
  103.8 1.2 copy-start.50
  143.4 29.7 %all-to-all-start = ((bf16[16,42,768]{2,1,0:T(8,128)(2,1)}), bf16[16,42,768]{2,1,0:T(8,128)(2,1)S(1)}, u32[]{:S(2)}, u32[]{:S(2)}) async-start(bf16[16,42,768]{2,1,0:T(8,128)(2,1)} %bitcast.86), calls=%async_computation | async-start | bytes 2359296 | tf_op jit(solution)/shard_map/all_to_all | solution.py:60
  174.2 4.7 copy-start.20
  177.9 1.0 copy-start.56
  180.9 31.8 %all-to-all-start.1 = ((bf16[16,42,768]{2,1,0:T(8,128)(2,1)}), bf16[16,42,768]{2,1,0:T(8,128)(2,1)S(1)}, u32[]{:S(2)}, u32[]{:S(2)}) async-start(bf16[16,42,768]{2,1,0:T(8,128)(2,1)} %convert_element_type.152), calls=%async_computation.1 | async-start | bytes 2359296 | tf_op jit(solution)/shard_map/all_to_all | solution.py:73
  191.9 27.0 %copy-start.52 = (s32[128]{0:T(128)S(1)}, s32[128]{0:T(128)}, u32[]{:S(2)}) copy-start(s32[128]{0:T(128)} %copy-done.51) | copy-start | bytes 1540
  212.7 32.0 %all-to-all-start.3 = ((bf16[16,42,768]{2,1,0:T(8,128)(2,1)}), bf16[16,42,768]{2,1,0:T(8,128)(2,1)}, u32[]{:S(2)}, u32[]{:S(2)}) async-start(bf16[16,42,768]{2,1,0:T(8,128)(2,1)} %convert_element_type.160), calls=%async_computation.3 | async-start | bytes 2359296 | tf_op jit(solution)/shard_map/all_to_all | solution.py:73
  218.8 49.7 %all-reduce.15.cloned.1.call-start = ((), (), s32[]{:S(2)}) async-start(), calls=%async_computation.7 | async-start | bytes 786432 | tf_op jit(solution)/shard_map/psum | solution.py:80
  247.0 1.0 copy-start.48
  247.0 2.1 copy-start.37
  247.0 21.4 %copy-start.10 = (bf16[128,768]{1,0:T(8,128)(2,1)S(1)}, bf16[128,768]{1,0:T(8,128)(2,1)}, u32[]{:S(2)}) copy-start(bf16[128,768]{1,0:T(8,128)(2,1)} %param.19) | copy-start | bytes 589828
  247.9 21.7 %copy-start.30 = (bf16[768,4]{0,1:T(4,128)(2,1)S(1)}, bf16[768,4]{0,1:T(4,128)(2,1)}, u32[]{:S(2)}) copy-start(bf16[768,4]{0,1:T(4,128)(2,1)} %param.31) | copy-start | bytes 18436
  247.9 21.7 %copy-start.32 = (s32[128,1]{0,1:T(1,128)S(1)}, s32[128,1]{0,1:T(1,128)}, u32[]{:S(2)}) copy-start(s32[128,1]{0,1:T(1,128)} %param.22) | copy-start | bytes 1540
  248.0 21.7 %copy-start.34 = (f32[128,4]{0,1:T(4,128)S(1)}, f32[128,4]{0,1:T(4,128)}, u32[]{:S(2)}) copy-start(f32[128,4]{0,1:T(4,128)} %get-tuple-element.30) | copy-start | bytes 6148
  248.0 21.7 %copy-start.39 = (f32[128]{0:T(128)S(1)}, f32[128]{0:T(128)}, u32[]{:S(2)}) copy-start(f32[128]{0:T(128)} %copy-done.38) | copy-start | bytes 1540
  248.0 21.7 %copy-start.47 = (f32[128]{0:T(128)S(1)}, f32[128]{0:T(128)}, u32[]{:S(2)}) copy-start(f32[128]{0:T(128)} %copy-done.46) | copy-start | bytes 1540
  248.9 51.2 %all-reduce.11.cloned.1.call-start = ((), (), s32[]{:S(2)}) async-start(), calls=%async_computation.5 | async-start | bytes 393216 | tf_op jit(solution)/shard_map/psum | solution.py:245
  268.5 2.6 copy-start.19
  269.6 1.4 copy-start.44
  269.7 3.0 copy-start.5
  269.7 3.0 copy-start.42
  272.6 0.9 copy-start.24
  273.1 0.9 copy-start.16
  273.5 0.9 copy-start.18
  273.5 1.1 copy-start.22
  273.5 1.1 copy-start.43
  274.0 2.0 copy-start.6
  274.6 1.7 copy-start.28
  276.0 1.8 copy-start.8
  280.7 208.5 %all-reduce.13.cloned.1.call-start = ((), (), s32[]{:S(2)}) async-start(), calls=%async_computation.6 | async-start | bytes 9437184 | tf_op jit(solution)/shard_map/psum | solution.py:248
  282.2 1.2 copy-start.14
  283.4 3.0 copy-start.2
  283.4 3.0 copy-start.57
  289.5 1.1 copy-start.55
  289.5 1.3 copy-start.33
  289.5 1.3 copy-start.35
  289.5 1.3 copy-start.40
  289.5 1.3 copy-start.45
  290.5 90.4 %copy-start.49 = (f32[128]{0:T(128)S(1)}, f32[128]{0:T(128)}, u32[]{:S(2)}) copy-start(f32[128]{0:T(128)} %get-tuple-element.37) | copy-start | bytes 1540
  489.2 2.5 copy-start.13
  491.6 1.7 copy-start.12
  493.3 1.7 copy-start.11
  (1 other events, 0.6 us)
Sparse Core Ops, SparseCore 0:
  78.2 21.1 all-reduce.8
  249.0 19.4 all-reduce.14
  280.8 19.2 all-reduce.10
  306.5 182.6 all-reduce.12
where the time goes:
time: 504 us; the launch traced here: 503 us
  waiting for transfers between devices  220 us (44%)
  blocking collectives  117 us (23%)
  local copies, waits for them, and re-layouts  88.8 us (18%)
  matrix products  29.4 us (6%)
  other arithmetic  16.8 us (3%)
  starting transfers between devices  16.3 us (3%)
  between operations  14.7 us (3%)
    psum x1, waiting for transfers between devices, local(): lax.psum((attn_gain_grad, query_grad, key_grad, value_grad, output_weight...  107 us
    psum x1, blocking collectives, local(): lax.psum((attn_gain_grad, query_grad, key_grad, value_grad, output_weight...  79.7 us
    gather x2, local copies, waits for them, and re-layouts, local(): bias = relative.T[:, offsets]  61.1 us
    all_to_all x2, waiting for transfers between devices, bring_back(): lax.all_to_all(shaped.astype(jnp.bfloat16), 'dp', split_axis=0, concat_ax...  44.6 us
    all_to_all x1, blocking collectives, send_out(): lax.all_to_all(copies.reshape(experts * quarter, capacity, width), 'dp',...  37.1 us
    all_to_all x1, waiting for transfers between devices, send_out(): lax.all_to_all(copies.reshape(experts * quarter, capacity, width), 'dp',...  20.7 us
    psum x1, waiting for transfers between devices, local(): attended = lax.psum(attn_part, 'tensor') * keep[:, None]  19.6 us
    psum x1, waiting for transfers between devices, bring_back(): return lax.psum(gathered.astype(jnp.bfloat16), 'tensor').astype(jnp.float32)  19.3 us
  transfers between devices with their start and end apart: 7, of which 7 were waited for; matrix products, arithmetic and copies ran while one was open for 5% of the time, Pallas kernels for 0%

commit v1 on v0

--- a/solution.py
+++ b/solution.py
@@ -1,6 +1,10 @@
+import functools
+
 import jax
 import jax.numpy as jnp
 from jax import lax
+from jax.experimental import pallas as pl
+from jax.experimental.pallas import tpu as pltpu
 from jax.sharding import PartitionSpec as P
 
 HEAD_DIM = 64
@@ -24,7 +28,8 @@
     device = lax.axis_index("dp")
     mine = (seq_owner == device).astype(jnp.int32)
     owned = mine * seq_lengths
-    starts = jnp.cumsum(owned) - owned
+    order = jnp.arange(owned.shape[0], dtype=jnp.int32)
+    starts = jnp.sum(jnp.where(order[None, :] < order[:, None], owned[None, :], 0), axis=1)
     slots = jnp.arange(rows, dtype=jnp.int32)
     inside = (
         (mine[:, None] > 0)
@@ -46,38 +51,384 @@
     return jnp.sum(flat.reshape(heads, length, 2 * length - 1), axis=1)
 
 
+MESH = pl.DeviceIdType.MESH
+LIMIT = 48 * 1024 * 1024
+
+
+def params(number):
+    return pltpu.CompilerParams(
+        collective_id=number, has_side_effects=True, vmem_limit_bytes=LIMIT
+    )
+
+
+def in_vmem(count):
+    return [pl.BlockSpec(memory_space=pltpu.VMEM)] * count
+
+
+def greet(peers):
+    barrier = pltpu.get_barrier_semaphore()
+    for peer in peers:
+        pl.semaphore_signal(barrier, inc=1, device_id=peer, device_id_type=MESH)
+    pl.semaphore_wait(barrier, len(peers))
+
+
+def remote(src, dst, send_sem, recv_sem, peer):
+    return pltpu.make_async_remote_copy(
+        src_ref=src,
+        dst_ref=dst,
+        send_sem=send_sem,
+        recv_sem=recv_sem,
+        device_id=peer,
+        device_id_type=MESH,
+    )
+
+
+def place(quarter):
+    device = lax.axis_index("dp")
+    return device // quarter, lax.rem(device, quarter), lax.axis_index("tensor")
+
+
+def pair_kernel(x_ref, out_ref, got, send_sem, recv_sem):
+    peer = (lax.axis_index("dp"), 1 - lax.axis_index("tensor"))
+    greet([peer])
+    copy = remote(x_ref, got, send_sem, recv_sem, peer)
+    copy.start()
+    copy.wait()
+    out_ref[...] = x_ref[...].astype(jnp.float32) + got[...].astype(jnp.float32)
+
+
+def pair_sum(x, number):
+    return pl.pallas_call(
+        pair_kernel,
+        out_shape=jax.ShapeDtypeStruct(x.shape, jnp.float32),
+        in_specs=in_vmem(1),
+        out_specs=in_vmem(1)[0],
+        scratch_shapes=[
+            pltpu.VMEM(x.shape, x.dtype),
+            pltpu.SemaphoreType.DMA,
+            pltpu.SemaphoreType.DMA,
+        ],
+        compiler_params=params(number),
+    )(x)
+
+
+def all_peers(experts, quarter, e, q, t):
+    lines = [(lax.rem(e + k, experts) * quarter + q, t) for k in range(1, experts)]
+    planes = [(e * quarter + lax.rem(q + m, quarter), t) for m in range(1, quarter)]
+    return [None] + lines, [None] + planes, (e * quarter + q, 1 - t)
+
+
+def dispatch_kernel(experts, quarter, picked, out, s1, r1, s2, r2, s3, r3):
+    e, q, t = place(quarter)
+    lines, planes, partner = all_peers(experts, quarter, e, q, t)
+    greet(lines[1:] + planes[1:] + [partner])
+    sent = []
+    hops = {}
+    for k in range(1, experts):
+        copy = remote(
+            picked.at[t, lax.rem(e + k, experts)], out.at[t, q, e], s1.at[k], r1.at[k], lines[k]
+        )
+        copy.start()
+        sent.append(copy)
+        hops[k] = copy
+    spread = {}
+    shared = []
+    for k in range(experts):
+        came = lax.rem(e - k + experts, experts)
+        if k == 0:
+            block = picked.at[t, e]
+            out[t, q, e] = picked[t, e]
+        else:
+            hops[k].wait_recv()
+            block = out.at[t, q, came]
+        for m in range(1, quarter):
+            copy = remote(block, out.at[t, q, came], s2.at[m, k], r2.at[m, k], planes[m])
+            copy.start()
+            sent.append(copy)
+            spread[m, k] = copy
+        copy = remote(block, out.at[t, q, came], s3.at[0, k], r3.at[0, k], partner)
+        copy.start()
+        sent.append(copy)
+        shared.append(copy)
+    for k in range(experts):
+        came = lax.rem(e - k + experts, experts)
+        for m in range(1, quarter):
+            side = lax.rem(q - m + quarter, quarter)
+            spread[m, k].wait_recv()
+            block = out.at[t, side, came]
+            copy = remote(block, block, s3.at[m, k], r3.at[m, k], partner)
+            copy.start()
+            sent.append(copy)
+            shared.append(copy)
+    for copy in shared:
+        copy.wait_recv()
+    for copy in sent:
+        copy.wait_send()
+
+
+def dispatch(picked, quarter):
+    _, experts, capacity, width = picked.shape
+    sems = [(experts,), (experts,)] + [(quarter, experts)] * 4
+    return pl.pallas_call(
+        functools.partial(dispatch_kernel, experts, quarter),
+        out_shape=jax.ShapeDtypeStruct((2, quarter, experts, capacity, width), picked.dtype),
+        in_specs=in_vmem(1),
+        out_specs=in_vmem(1)[0],
+        scratch_shapes=[pltpu.SemaphoreType.DMA(shape) for shape in sems],
+        compiler_params=params(2),
+    )(picked)
+
+
+def collect_kernel(
+    experts, quarter, part, out, got0, sum0, got1, acc, low, s0, r0, s1, r1, s2, r2, s3, r3
+):
+    e, q, t = place(quarter)
+    lines, planes, partner = all_peers(experts, quarter, e, q, t)
+    greet(lines[1:] + planes[1:] + [partner])
+    sent = []
+    firsts = {}
+    order = list(range(1, quarter)) + [0]
+    for m in order:
+        side = lax.rem(q + m, quarter)
+        copy = remote(part.at[1 - t, side], got0.at[m], s0.at[m], r0.at[m], partner)
+        copy.start()
+        sent.append(copy)
+        firsts[m] = copy
+    seconds = {}
+    for m in order:
+        side = lax.rem(q + m, quarter)
+        firsts[m].wait_recv()
+        total = part[t, side].astype(jnp.float32) + got0[m].astype(jnp.float32)
+        if m == 0:
+            acc[...] = total
+        else:
+            sum0[m] = total.astype(jnp.bfloat16)
+            copy = remote(sum0.at[m], got1.at[m], s1.at[m], r1.at[m], planes[m])
+            copy.start()
+            sent.append(copy)
+            seconds[m] = copy
+    for m in range(1, quarter):
+        seconds[m].wait_recv()
+    total = acc[...]
+    for m in range(1, quarter):
+        total = total + got1[m].astype(jnp.float32)
+    low[...] = total.astype(jnp.bfloat16)
+    thirds = {}
+    for k in range(1, experts):
+        copy = remote(
+            low.at[lax.rem(e + k, experts)], out.at[t, e], s2.at[k], r2.at[k], lines[k]
+        )
+        copy.start()
+        sent.append(copy)
+        thirds[k] = copy
+    out[t, e] = low[e]
+    shared = []
+    for k in range(experts):
+        came = lax.rem(e - k + experts, experts)
+        if k == 0:
+            block = low.at[e]
+        else:
+            thirds[k].wait_recv()
+            block = out.at[t, came]
+        copy = remote(block, out.at[t, came], s3.at[k], r3.at[k], partner)
+        copy.start()
+        sent.append(copy)
+        shared.append(copy)
+    for copy in shared:
+        copy.wait_recv()
+    for copy in sent:
+        copy.wait_send()
+
+
+def collect(part):
+    _, quarter, experts, capacity, width = part.shape
+    low = part.dtype
+    block = (experts, capacity, width)
+    sems = [(quarter,)] * 4 + [(experts,)] * 4
+    return pl.pallas_call(
+        functools.partial(collect_kernel, experts, quarter),
+        out_shape=jax.ShapeDtypeStruct((2, experts, capacity, width), low),
+        in_specs=in_vmem(1),
+        out_specs=in_vmem(1)[0],
+        scratch_shapes=[
+            pltpu.VMEM((quarter,) + block, low),
+            pltpu.VMEM((quarter,) + block, low),
+            pltpu.VMEM((quarter,) + block, low),
+            pltpu.VMEM(block, jnp.float32),
+            pltpu.VMEM(block, low),
+        ]
+        + [pltpu.SemaphoreType.DMA(shape) for shape in sems],
+        compiler_params=params(3),
+    )(part)
+
+
+def reduce_kernel(
+    experts, quarter, g, small, out, small_out,
+    got1, sum1, got2, tiny1, mid, tiny2,
+    s1, r1, s2, r2, s3, r3, s4, r4, s5, r5, s6, r6,
+):
+    e, q, t = place(quarter)
+    lines, planes, _ = all_peers(experts, quarter, e, q, t)
+    greet(lines[1:] + planes[1:])
+    sent = []
+    tiny = []
+    for m in range(1, quarter):
+        copy = remote(small, tiny1.at[q], s5.at[m], r5.at[m], planes[m])
+        copy.start()
+        sent.append(copy)
+        tiny.append(copy)
+    tiny1[q] = small[...]
+    order = list(range(1, experts)) + [0]
+    firsts = {}
+    for k in order:
+        for m in range(1, quarter):
+            copy = remote(
+                g.at[lax.rem(q + m, quarter), lax.rem(e + k, experts)],
+                got1.at[m, k],
+                s1.at[m, k],
+                r1.at[m, k],
+                planes[m],
+            )
+            copy.start()
+            sent.append(copy)
+            firsts[m, k] = copy
+    for copy in tiny:
+        copy.wait_recv()
+    total = tiny1[0]
+    for m in range(1, quarter):
+        total = total + tiny1[m]
+    mid[...] = total
+    tiny2[e] = total
+    tiny = []
+    for k in range(1, experts):
+        copy = remote(mid, tiny2.at[e], s6.at[k], r6.at[k], lines[k])
+        copy.start()
+        sent.append(copy)
+        tiny.append(copy)
+    seconds = {}
+    for k in order:
+        total = g[q, lax.rem(e + k, experts)].astype(jnp.float32)
+        for m in range(1, quarter):
+            firsts[m, k].wait_recv()
+            total = total + got1[m, k].astype(jnp.float32)
+        if k > 0:
+            sum1[k] = total.astype(jnp.bfloat16)
+            copy = remote(sum1.at[k], got2.at[k], s2.at[k], r2.at[k], lines[k])
+            copy.start()
+            sent.append(copy)
+            seconds[k] = copy
+    for k in range(1, experts):
+        seconds[k].wait_recv()
+        total = total + got2[k].astype(jnp.float32)
+    sum1[0] = total.astype(jnp.bfloat16)
+    out[q, e] = total.astype(jnp.bfloat16)
+    thirds = {}
+    for k in range(1, experts):
+        copy = remote(sum1.at[0], out.at[q, e], s3.at[k], r3.at[k], lines[k])
+        copy.start()
+        sent.append(copy)
+        thirds[k] = copy
+    last = []
+    for k in range(experts):
+        came = lax.rem(e - k + experts, experts)
+        if k == 0:
+            block = sum1.at[0]
+        else:
+            thirds[k].wait_recv()
+            block = out.at[q, came]
+        for m in range(1, quarter):
+            copy = remote(block, out.at[q, came], s4.at[m, k], r4.at[m, k], planes[m])
+            copy.start()
+            sent.append(copy)
+            last.append(copy)
+    for copy in tiny:
+        copy.wait_recv()
+    total = tiny2[0]
+    for k in range(1, experts):
+        total = total + tiny2[k]
+    small_out[...] = total
+    for copy in last:
+        copy.wait_recv()
+    for copy in sent:
+        copy.wait_send()
+
+
+def reduce_all(g, small):
+    quarter, experts, piece, width = g.shape
+    low = g.dtype
+    both = (quarter, experts)
+    sems = [both, both] + [(experts,)] * 4 + [both, both] + [(quarter,)] * 2 + [(experts,)] * 2
+    return pl.pallas_call(
+        functools.partial(reduce_kernel, experts, quarter),
+        out_shape=(
+            jax.ShapeDtypeStruct(g.shape, low),
+            jax.ShapeDtypeStruct(small.shape, jnp.float32),
+        ),
+        in_specs=in_vmem(2),
+        out_specs=tuple(in_vmem(2)),
+        scratch_shapes=[
+            pltpu.VMEM(g.shape, low),
+            pltpu.VMEM((experts, piece, width), low),
+            pltpu.VMEM((experts, piece, width), low),
+            pltpu.VMEM((quarter,) + small.shape, jnp.float32),
+            pltpu.VMEM(small.shape, jnp.float32),
+            pltpu.VMEM((experts,) + small.shape, jnp.float32),
+        ]
+        + [pltpu.SemaphoreType.DMA(shape) for shape in sems],
+        compiler_params=params(4),
+    )(g, small)
+
+
+def bias_kernel(rows, relative, out):
+    span = relative.shape[1]
+    for head in range(out.shape[0]):
+        wide = jnp.broadcast_to(relative[head : head + 1, :], (rows, span))
+        turned = pltpu.roll(wide, span - rows + 1, 1, stride=1, stride_axis=0)
+        out[head] = turned[:, :rows]
+
+
+def bias_of(relative, rows):
+    heads = relative.shape[1]
+    span = 2 * rows
+    wide = jnp.pad(relative.T, ((0, 0), (0, span - relative.shape[0])))
+    return pl.pallas_call(
+        functools.partial(bias_kernel, rows),
+        out_shape=jax.ShapeDtypeStruct((heads, rows, rows), jnp.float32),
+        in_specs=in_vmem(1),
+        out_specs=in_vmem(1)[0],
+    )(wide)
+
+
+def rows_up(amount, step):
+    return (amount + step - 1) // step * step
+
+
+def reduce_grads(large, small, experts, quarter):
+    width = large[0].shape[1]
+    stack = jnp.concatenate([one.astype(jnp.bfloat16) for one in large], axis=0)
+    rows = stack.shape[0]
+    piece = rows_up(-(-rows // (experts * quarter)), 16)
+    stack = jnp.pad(stack, ((0, piece * experts * quarter - rows), (0, 0)))
+    flat = jnp.concatenate([one.reshape(-1) for one in small])
+    amount = flat.shape[0]
+    flat = jnp.pad(flat, (0, rows_up(amount, 1024) - amount)).reshape(-1, 128)
+    done, tiny = reduce_all(stack.reshape(quarter, experts, piece, width), flat)
+    done = done.reshape(-1, width)
+    tiny = tiny.reshape(-1)
+    wide, at = [], 0
+    for one in large:
+        wide.append(done[at : at + one.shape[0]].astype(jnp.float32))
+        at += one.shape[0]
+    thin, at = [], 0
+    for one in small:
+        thin.append(tiny[at : at + one.size].reshape(one.shape))
+        at += one.size
+    return wide, thin
+
+
 def scores_of(queries, keys, bias, allowed):
     raw = jnp.einsum("ihc,jhc->hij", queries, keys, preferred_element_type=jnp.float32) + bias
     return jnp.where(allowed[None], raw, -1e30)
-
-
-def send_out(rows_low, source, filled, experts, quarter, capacity):
-    width = rows_low.shape[1]
-    picked = jnp.where(filled[:, None], rows_low[source], jnp.zeros((), rows_low.dtype))
-    copies = jnp.broadcast_to(
-        picked.reshape(experts, 1, capacity, width), (experts, quarter, capacity, width)
-    )
-    arrived = lax.all_to_all(
-        copies.reshape(experts * quarter, capacity, width),
-        "dp",
-        split_axis=0,
-        concat_axis=0,
-        tiled=True,
-    )
-    return arrived.reshape(experts * quarter * capacity, width)
-
-
-def bring_back(part, slot, experts, quarter, capacity):
-    width = part.shape[1]
-    shaped = part.reshape(experts * quarter, capacity, width)
-    returned = lax.all_to_all(
-        shaped.astype(jnp.bfloat16), "dp", split_axis=0, concat_axis=0, tiled=True
-    ).astype(shaped.dtype)
-    table = jnp.sum(returned.reshape(experts, quarter, capacity, width), axis=1).reshape(
-        experts * capacity, width
-    )
-    gathered = jnp.take(table, slot, axis=0, mode="fill", fill_value=0.0)
-    return lax.psum(gathered.astype(jnp.bfloat16), "tensor").astype(jnp.float32)
 
 
 def expert_forward(arrived, expert_in, expert_out):
@@ -118,7 +469,7 @@
     experts = router_weight.shape[1]
     groups = lax.axis_size("dp")
     quarter = groups // experts
-    capacity = max(2, 4 * rows // (3 * experts))
+    capacity = rows_up(max(2, 4 * rows // (3 * experts)), 16)
     segment, valid = block_layout(seq_lengths, seq_owner, rows)
     keep = valid.astype(jnp.float32)
     inputs = tokens.astype(jnp.float32)
@@ -140,12 +491,11 @@
         .reshape(rows, local_heads, HEAD_DIM)
     )
     positions = jnp.arange(rows, dtype=jnp.int32)
-    offsets = positions[None, :] - positions[:, None] + rows - 1
     lookup = (
         rel_buckets[:, None] == jnp.arange(bias_table.shape[0], dtype=jnp.int32)[None, :]
     ).astype(jnp.float32)
     relative = jnp.dot(lookup, bias_table, precision=lax.Precision.HIGHEST)
-    bias = relative.T[:, offsets]
+    bias = bias_of(relative, rows)
     allowed = (segment[:, None] == segment[None, :]) & valid[:, None] | (
         positions[:, None] == positions[None, :]
     )
@@ -161,7 +511,7 @@
         .reshape(rows, -1)
     )
     attn_part = jnp.dot(mixed, output_weight, preferred_element_type=jnp.float32)
-    attended = lax.psum(attn_part, "tensor") * keep[:, None]
+    attended = pair_sum(attn_part, 0) * keep[:, None]
     middle = inputs + attended
     normed_two_full, scale_two = rms_rows(middle, ffn_gain)
     normed_two = normed_two_full.astype(jnp.bfloat16)
@@ -172,20 +522,34 @@
     route_hot = chosen[:, None] == expert_ids[None, :]
     gate = jnp.sum(gate_probs * route_hot.astype(jnp.float32), axis=-1)
     picked = (route_hot & valid[:, None]).astype(jnp.int32)
-    rank = jnp.sum((jnp.cumsum(picked, axis=0) - picked) * picked, axis=1)
+    before = (positions[None, :] < positions[:, None]).astype(jnp.bfloat16)
+    ahead = jnp.dot(before, picked.astype(jnp.bfloat16), preferred_element_type=jnp.float32)
+    rank = jnp.sum(ahead.astype(jnp.int32) * picked, axis=1)
     slot = jnp.where(valid, chosen * capacity + rank, experts * capacity)
     places = jnp.arange(experts * capacity, dtype=jnp.int32)
     match = slot[None, :] == places[:, None]
-    source = jnp.sum(match.astype(jnp.int32) * positions[None, :], axis=1)
-    filled = jnp.any(match, axis=1)
+    chooser = match.astype(jnp.bfloat16)
     grad_out = cotangent.astype(jnp.float32)
     expert_grad = (gate[:, None] * grad_out).astype(jnp.bfloat16)
-    arrived = send_out(normed_two, source, filled, experts, quarter, capacity)
+    width = tokens.shape[1]
+    chosen_rows = jnp.dot(
+        chooser,
+        jnp.concatenate([normed_two, expert_grad], axis=1),
+        preferred_element_type=jnp.float32,
+    ).astype(jnp.bfloat16)
+    shipped = jnp.stack([chosen_rows[:, :width], chosen_rows[:, width:]])
+    landed = dispatch(shipped.reshape(2, experts, capacity, width), quarter)
+    landed = landed.reshape(2, groups * capacity, width)
+    arrived, arrived_grad = landed[0], landed[1]
     act, gelu_back, part = expert_forward(arrived, expert_in, expert_out)
-    expert_rows = bring_back(part, slot, experts, quarter, capacity)
-    arrived_grad = send_out(expert_grad, source, filled, experts, quarter, capacity)
     pre_grad, input_part = expert_backward(arrived_grad, gelu_back, expert_in, expert_out)
-    expert_input_grad = bring_back(input_part, slot, experts, quarter, capacity)
+    partial = jnp.stack([part.astype(jnp.bfloat16), input_part.astype(jnp.bfloat16)])
+    returned = collect(partial.reshape(2, quarter, experts, capacity, width))
+    returned = returned.reshape(2, experts * capacity, width)
+    back = jnp.einsum(
+        "pt,apd->atd", chooser, returned, preferred_element_type=jnp.float32
+    )
+    expert_rows, expert_input_grad = back[0], back[1]
     output = (middle + gate[:, None] * expert_rows).astype(jnp.bfloat16)
     gate_grad = jnp.sum(grad_out * expert_rows, axis=-1)
     logit_grad = (
@@ -242,21 +606,26 @@
         + jnp.einsum("tc,dc->td", keys_grad, key_weight, preferred_element_type=jnp.float32)
         + jnp.einsum("tc,dc->td", values_grad, value_weight, preferred_element_type=jnp.float32)
     )
-    normed_grad = lax.psum(normed_part.astype(jnp.bfloat16), "tensor").astype(jnp.float32)
+    normed_grad = pair_sum(normed_part.astype(jnp.bfloat16), 1)
     input_part_grad, attn_gain_grad = rms_back(inputs, attn_gain, scale_one, normed_grad)
     tokens_grad = (middle_grad + input_part_grad).astype(jnp.bfloat16)
-    summed = lax.psum(
-        (
-            attn_gain_grad,
-            query_grad,
-            key_grad,
-            value_grad,
-            output_weight_grad,
-            table_grad,
-            ffn_gain_grad,
-            router_grad,
-        ),
-        "dp",
+    half = output_weight_grad.shape[0]
+    pieces = [output_weight_grad[:, at : at + half] for at in range(0, width, half)]
+    wide, thin = reduce_grads(
+        [query_grad, key_grad, value_grad] + pieces,
+        [attn_gain_grad, table_grad, ffn_gain_grad, router_grad],
+        experts,
+        quarter,
+    )
+    summed = (
+        thin[0],
+        wide[0],
+        wide[1],
+        wide[2],
+        jnp.concatenate(wide[3:], axis=1),
+        thin[1],
+        thin[2],
+        thin[3],
     )
     return (
         output,

time: 504 us -> 158 us (0.31)
  waiting for transfers between devices: 220 us -> 0 us
  blocking collectives: 117 us -> 0 us
  Pallas kernels: 0 us -> 113 us
  local copies, waits for them, and re-layouts: 88.8 us -> 11 us
  starting transfers between devices: 16.3 us -> 0 us
  between operations: 14.7 us -> 1.3 us
  matrix products: 29.4 us -> 21.6 us
  other arithmetic: 16.8 us -> 10.8 us
    psum x4 -> x0, waiting for transfers between devices: 154 us -> none  [the longest x1 107 us: local(): lax.psum((attn_gain_grad, query_grad, key_grad, value_grad, output_weight...]
    pallas_call x0 -> x6, Pallas kernels: none -> 113 us  [the longest x1 58.8 us: reduce_all(): pl.pallas_call(functools.partial(reduce_kernel, experts, quarter), out_sh...]
    psum x1 -> x0, blocking collectives: 79.7 us -> none  [local(): lax.psum((attn_gain_grad, query_grad, key_grad, value_grad, output_weight...]
    all_to_all x3 -> x0, waiting for transfers between devices: 65.3 us -> none  [the longest x2 44.6 us: bring_back(): lax.all_to_all(shaped.astype(jnp.bfloat16), 'dp', split_axis=0, concat_ax...]
    gather x8 -> x0, local copies, waits for them, and re-layouts: 64.9 us -> none  [the longest x2 61.1 us: local(): bias = relative.T[:, offsets]]
    all_to_all x1 -> x0, blocking collectives: 37.1 us -> none  [send_out(): lax.all_to_all(copies.reshape(experts * quarter, capacity, width), 'dp',...]
    all_to_all x3 -> x0, starting transfers between devices: 15.9 us -> none  [the longest x2 12.2 us: bring_back(): lax.all_to_all(shaped.astype(jnp.bfloat16), 'dp', split_axis=0, concat_ax...]
    unnamed x123 -> x43, local copies, waits for them, and re-layouts: 11.9 us -> 3.85 us
  transfers between devices with their start and end apart: 7 -> 0, of which waited for: 7 -> 0; matrix products, arithmetic and copies ran while one was open for 5% -> 0% of each run, Pallas kernels for 0% -> 0%
where the time goes in v1:
time: 158 us
  Pallas kernels  113 us (72%)
  matrix products  21.6 us (14%)
  local copies, waits for them, and re-layouts  11 us (7%)
  other arithmetic  10.8 us (7%)
    pallas_call x1, Pallas kernels, reduce_all(): pl.pallas_call(functools.partial(reduce_kernel, experts, quarter), out_sh...  58.8 us
    pallas_call x1, Pallas kernels, collect(): pl.pallas_call(functools.partial(collect_kernel, experts, quarter), out_s...  27.4 us
    pallas_call x1, Pallas kernels, dispatch(): pl.pallas_call(functools.partial(dispatch_kernel, experts, quarter), out_...  21.7 us
    unnamed x43, local copies, waits for them, and re-layouts  3.85 us
    slice x5, local copies, waits for them, and re-layouts, reduce_grads(): thin.append(tiny[at:at + one.size].reshape(one.shape))  3.79 us
    pallas_call x2, Pallas kernels, pair_sum(): pl.pallas_call(pair_kernel, out_shape=jax.ShapeDtypeStruct(x.shape, jnp.f...  3.4 us

profile of v1, /device:TPU:0, one launch (start us, length us, event | category | flops | bytes accessed | tf_op | source)
XLA Modules:
  0.0 157.8 jit_solution(5528812648825489750)
XLA Ops:
  0.7 0.8 compare_select_fusion
  1.5 0.7 fusion.52
  2.4 1.1 fusion.16
  3.4 0.9 fusion.13
  4.3 0.7 add_select_fusion
  5.0 0.9 convolution_bitcast_fusion.1
  5.9 0.7 pad.12.relative
  6.7 1.5 convolution_convert_fusion.9
  8.3 0.3 convolution_convert_fusion.8
  8.8 0.3 convolution_convert_fusion.10
  9.3 1.7 %shard_map.247 = f32[6,128,128]{2,1,0:T(8,128)} custom-call(f32[6,256]{1,0:T(8,128)} %pad.12.relative), custom_call_target="tpu_custom_call" | custom-call | tf_op jit(solution)/shard_map/pallas_call | solution.py:394
  11.0 1.4 fusion.67
  12.3 0.3 fusion.30
  12.7 0.4 convolution_convert_fusion.14
  13.1 0.3 copy-done.4
  13.4 0.3 fusion.70.x_ref
  13.7 1.9 %shard_map.248 = f32[128,768]{1,0:T(8,128)S(1)} custom-call(f32[128,768]{1,0:T(8,128)S(1)} %fusion.70.x_ref), custom_call_target="tpu_custom_call" | custom-call | tf_op jit(solution)/shard_map/pallas_call | solution.py:101
  15.6 0.2 multiply_reduce_fusion.3
  16.3 0.3 convolution_convert_fusion
  16.8 21.7 %shard_map.249 = bf16[2,4,4,48,768]{4,3,2,1,0:T(8,128)(2,1)S(1)} custom-call(bf16[2,4,48,768]{3,2,1,0:T(8,128)(2,1)S(1)} %pad_maximum_fusion.1.picked), custom_call_target="tpu_custom_call" | custom-call | tf_op jit(solution)/shard_map/pallas_call | solution.py:172
  38.7 0.9 copy-done.10
  39.6 0.8 fusion.71
  40.4 1.4 fusion.10
  41.8 1.8 %fusion.73 = f32[768,384]{1,0:T(8,128)} fusion(bf16[768,768]{1,0:T(8,128)(2,1)S(1)} %bitcast.114, bf16[768,384]{1,0:T(8,128)(2,1)S(1)} %get-tuple-element.73), kind=kOutput, calls=%fused_computation.147 | convolution fusion | flops 452984832 | bytes 2949120 | tf_op jit(solution)/shard_map/rd,rf->df/dot_general | solution.py:562
  43.6 1.8 %fusion.55 = f32[384,768]{1,0:T(8,128)} fusion(bf16[768,768]{1,0:T(8,128)(2,1)S(1)} %bitcast.111, f32[768,384]{1,0:T(8,128)S(1)} %get-tuple-element.74), kind=kOutput, calls=%fused_computation.136 | convolution fusion | flops 455639040 | bytes 3538944 | tf_op jit(solution)/shard_map/rf,rd->fd/dot_general | solution.py:561
  45.4 0.9 convolution_convert_fusion.2
  46.3 0.8 convolution_convert_fusion.1
  47.1 0.2 pad_maximum_fusion.part
  47.3 27.4 %shard_map.250 = bf16[2,4,48,768]{3,2,1,0:T(8,128)(2,1)S(1)} custom-call(bf16[2,4,4,48,768]{4,3,2,1,0:T(8,128)(2,1)S(1)} %pad_maximum_fusion.part), custom_call_target="tpu_custom_call" | custom-call | tf_op jit(solution)/shard_map/pallas_call | solution.py:248
  74.8 0.3 convolution_bitcast_fusion
  75.1 0.8 fusion.15
  75.9 0.4 multiply_reduce_fusion
  76.4 0.3 convolution_convert_fusion.7
  76.9 0.3 convolution_convert_fusion.11
  77.2 0.2 fusion.69
  77.5 0.2 reshape.259
  77.7 0.4 multiply_reduce_fusion.1
  78.1 0.3 multiply_convert_fusion.1
  78.4 0.8 convolution_convert_fusion.12
  79.2 0.9 convolution_convert_fusion.13
  80.3 0.5 copy.70
  80.9 1.0 reshape.257
  82.0 0.3 fusion.37
  82.4 0.5 copy-done.5
  82.9 1.3 fusion.72
  84.2 0.3 convolution_add_fusion.2
  84.6 0.3 fusion.11.x_ref
  84.9 1.5 shard_map.251
  86.7 0.9 fusion.22
  87.6 0.4 convolution_convert_fusion.3
  88.0 0.4 fusion
  88.4 0.5 fusion.1
  88.9 0.5 fusion.2
  89.5 58.8 %shard_map.252 = (bf16[4,4,192,384]{3,2,1,0:T(8,128)(2,1)S(1)}, f32[40,128]{1,0:T(8,128)S(1)}) custom-call(bf16[4,4,192,384]{3,2,1,0:T(8,128)(2,1)S(1)} %bitcast.105, f32[40,128]{1,0:T(8,128)S(1)} %pad_bitcast_fusion.1.small), custom_call_target="tpu_custom_call" | custom-call | tf_op jit(solution)/shard_map/pallas_call | solution.py:361
  148.3 0.7 slice.97
  149.0 0.6 slice_bitcast_fusion.2
  149.7 0.7 copy.63
  150.4 1.1 maximum_convert_fusion
  151.5 1.5 slice.85
  153.0 1.0 slice.98
  154.0 0.8 copy.64
  154.8 0.2 fusion.64
  155.0 1.1 bitcast_convert_fusion.2
  156.1 1.7 %bitcast_convert_fusion = (f32[768,384]{1,0:T(8,128)}, f32[768,384]{1,0:T(8,128)}) fusion(bf16[1,4,192,384]{3,2,1,0:T(8,128)(2,1)S(1)} %get-tuple-element.52, bf16[1,4,192,384]{3,2,1,0:T(8,128)(2,1)S(1)} %get-tuple-element.53), kind=kLoop, calls=%fused_computation.52 | loop fusion | flops 589824 | bytes 3538944 | tf_op jit(solution)/shard_map/convert_element_type | solution.py:420
  (71 shorter events, 2.8 us)
Async XLA Ops:
  0.6 39.7 %copy-start = (bf16[768,384]{1,0:T(8,128)(2,1)S(1)}, bf16[768,384]{1,0:T(8,128)(2,1)}, u32[]{:S(2)}) copy-start(bf16[768,384]{1,0:T(8,128)(2,1)} %param.30) | copy-start | bytes 1769476
  0.7 7.7 %copy-start.1 = (bf16[128,768]{1,0:T(8,128)(2,1)S(1)}, bf16[128,768]{1,0:T(8,128)(2,1)}, u32[]{:S(2)}) copy-start(bf16[128,768]{1,0:T(8,128)(2,1)} %param.16) | copy-start | bytes 589828
  0.7 7.7 %copy-start.14 = (f32[768]{0:T(1024)S(1)}, f32[768]{0:T(1024)}, u32[]{:S(2)}) copy-start(f32[768]{0:T(1024)} %param.22) | copy-start | bytes 9220
  0.7 7.6 %copy-start.6 = (bf16[768,384]{1,0:T(8,128)(2,1)S(1)}, bf16[768,384]{1,0:T(8,128)(2,1)}, u32[]{:S(2)}) copy-start(bf16[768,384]{1,0:T(8,128)(2,1)} %param.24) | copy-start | bytes 1769476
  3.4 5.4 %copy-start.2 = (bf16[768,384]{1,0:T(8,128)(2,1)S(1)}, bf16[768,384]{1,0:T(8,128)(2,1)}, u32[]{:S(2)}) copy-start(bf16[768,384]{1,0:T(8,128)(2,1)} %param.25) | copy-start | bytes 1769476
  12.3 1.1 copy-start.4
  13.1 2.7 %copy-start.12 = (bf16[6,64,128]{2,1,0:T(8,128)(2,1)}, bf16[6,64,128]{2,1,0:T(8,128)(2,1)S(1)}, u32[]{:S(2)}) copy-start(bf16[6,64,128]{2,1,0:T(8,128)(2,1)S(1)} %convolution_convert_fusion.14) | copy-start | bytes 294916
  13.4 2.4 %copy-start.15 = (f32[768]{0:T(1024)S(1)}, f32[768]{0:T(1024)}, u32[]{:S(2)}) copy-start(f32[768]{0:T(1024)} %param.28) | copy-start | bytes 9220
  13.7 2.3 %copy-start.16 = (bf16[768,4]{0,1:T(4,128)(2,1)S(1)}, bf16[768,4]{0,1:T(4,128)(2,1)}, u32[]{:S(2)}) copy-start(bf16[768,4]{0,1:T(4,128)(2,1)} %param.29) | copy-start | bytes 18436
  13.7 2.5 %copy-start.17 = (s32[128,1]{0,1:T(1,128)S(1)}, s32[128,1]{0,1:T(1,128)}, u32[]{:S(2)}) copy-start(s32[128,1]{0,1:T(1,128)} %param.20) | copy-start | bytes 1540
  13.7 2.5 %copy-start.8 = (bf16[128,768]{1,0:T(8,128)(2,1)S(1)}, bf16[128,768]{1,0:T(8,128)(2,1)}, u32[]{:S(2)}) copy-start(bf16[128,768]{1,0:T(8,128)(2,1)} %param.17) | copy-start | bytes 589828
  38.5 1.1 copy-start.10
  80.9 1.1 copy-start.18
  81.8 1.1 copy-start.5
  81.9 2.3 %copy-start.7 = (bf16[768,384]{1,0:T(8,128)(2,1)S(1)}, bf16[768,384]{1,0:T(8,128)(2,1)}, u32[]{:S(2)}) copy-start(bf16[768,384]{1,0:T(8,128)(2,1)} %param.24) | copy-start | bytes 1769476
  81.9 2.3 %copy-start.9 = (bf16[6,64,128]{2,1,0:T(8,128)(2,1)S(1)}, bf16[6,64,128]{2,1,0:T(8,128)(2,1)}, u32[]{:S(2)}) copy-start(bf16[6,64,128]{2,1,0:T(8,128)(2,1)} %convolution_convert_fusion.12) | copy-start | bytes 294916
  82.9 1.7 %copy-start.3 = (bf16[768,384]{1,0:T(8,128)(2,1)S(1)}, bf16[768,384]{1,0:T(8,128)(2,1)}, u32[]{:S(2)}) copy-start(bf16[768,384]{1,0:T(8,128)(2,1)} %param.25) | copy-start | bytes 1769476
  84.9 2.7 %copy-start.13 = (bf16[6,64,128]{2,1,0:T(8,128)(2,1)S(1)}, bf16[6,64,128]{2,1,0:T(8,128)(2,1)}, u32[]{:S(2)}) copy-start(bf16[6,64,128]{2,1,0:T(8,128)(2,1)} %copy-done.12) | copy-start | bytes 294916
  86.6 1.3 copy-start.11

commit v2 on v1

--- a/solution.py
+++ b/solution.py
@@ -112,16 +112,130 @@
     )(x)
 
 
-def all_peers(experts, quarter, e, q, t):
-    lines = [(lax.rem(e + k, experts) * quarter + q, t) for k in range(1, experts)]
-    planes = [(e * quarter + lax.rem(q + m, quarter), t) for m in range(1, quarter)]
-    return [None] + lines, [None] + planes, (e * quarter + q, 1 - t)
-
-
-def dispatch_kernel(experts, quarter, picked, out, s1, r1, s2, r2, s3, r3):
+def line_peers(experts, quarter, e, q, t):
+    return [None] + [(lax.rem(e + k, experts) * quarter + q, t) for k in range(1, experts)]
+
+
+def plane_of(quarter, e, q, t):
+    y, x = q // 2, lax.rem(q, 2)
+    beside = 2 * y + (1 - x)
+    below = 2 * (1 - y) + x
+    across = 2 * (1 - y) + (1 - x)
+    return (beside, below, across), (e * quarter + beside, t), (e * quarter + below, t)
+
+
+def part_of(ref, index, side):
+    half = ref.shape[-1] // 2
+    return ref.at[index + (slice(None), pl.ds(side * half, half))]
+
+
+def scatter_plane(g, ready, done, experts, e, q, sides, near, got, relay, got2, s1, r1, s2, r2):
+    beside, below, across = sides
+    first = near
+    second = (near[1], near[0])
+    keeps = (beside, below)
+    passes = (below, beside)
+    order = list(range(1, experts)) + [0]
+    sent = []
+    firsts = {}
+    seconds = {}
+    for k in order:
+        ed = lax.rem(e + k, experts)
+        ready(k, ed)
+        for j, piece_of in ((0, lambda i: across), (1, lambda i: keeps[i])):
+            for i in range(2):
+                copy = remote(
+                    part_of(g, (piece_of(i), ed), i),
+                    got.at[i, k, j],
+                    s1.at[i, k, j],
+                    r1.at[i, k, j],
+                    first[i],
+                )
+                copy.start()
+                sent.append(copy)
+                firsts[i, k, j] = copy
+
+    def finish(k):
+        ed = lax.rem(e + k, experts)
+        totals = []
+        for i in range(2):
+            firsts[i, k, 1].wait_recv()
+            seconds[i, k].wait_recv()
+            totals.append(
+                part_of(g, (q, ed), i)[...].astype(jnp.float32)
+                + got[i, k, 1].astype(jnp.float32)
+                + got2[i, k].astype(jnp.float32)
+            )
+        done(k, ed, totals)
+
+    for at, k in enumerate(order):
+        ed = lax.rem(e + k, experts)
+        for i in range(2):
+            firsts[i, k, 0].wait_recv()
+            relay[i, k] = (
+                part_of(g, (passes[i], ed), i)[...].astype(jnp.float32)
+                + got[i, k, 0].astype(jnp.float32)
+            ).astype(jnp.bfloat16)
+            copy = remote(relay.at[i, k], got2.at[i, k], s2.at[i, k], r2.at[i, k], second[i])
+            copy.start()
+            sent.append(copy)
+            seconds[i, k] = copy
+        if at > 0:
+            finish(order[at - 1])
+    finish(order[-1])
+    return sent
+
+
+def plane_scratch(experts, block, low):
+    half = (block[0], block[1] // 2)
+    return [
+        pltpu.VMEM((2, experts, 2) + half, low),
+        pltpu.VMEM((2, experts) + half, low),
+        pltpu.VMEM((2, experts) + half, low),
+        pltpu.SemaphoreType.DMA((2, experts, 2)),
+        pltpu.SemaphoreType.DMA((2, experts, 2)),
+        pltpu.SemaphoreType.DMA((2, experts)),
+        pltpu.SemaphoreType.DMA((2, experts)),
+    ]
+
+
+def gather_plane(out, lead, blocks, experts, e, q, sides, near, arrived, s1, r1, s2, r2):
+    beside, below, across = sides
+    sent = []
+    firsts = {}
+    for k in range(experts):
+        came = lax.rem(e - k + experts, experts)
+        block = blocks(k, came)
+        for i in range(2):
+            copy = remote(block, out.at[lead + (q, came)], s1.at[i, k], r1.at[i, k], near[i])
+            copy.start()
+            sent.append(copy)
+            firsts[i, k] = copy
+    seconds = {}
+    for k in range(experts):
+        came = lax.rem(e - k + experts, experts)
+        for i in range(2):
+            firsts[i, k].wait_recv()
+            ref = part_of(out, lead + ((beside, below)[i], came), i)
+            copy = remote(ref, ref, s2.at[i, k], r2.at[i, k], near[1 - i])
+            copy.start()
+            sent.append(copy)
+            seconds[i, k] = copy
+            arrived(out.at[lead + ((beside, below)[i], came)], i, k)
+    for k in range(experts):
+        came = lax.rem(e - k + experts, experts)
+        for i in range(2):
+            seconds[i, k].wait_recv()
+        arrived(out.at[lead + (across, came)], 2, k)
+    return sent
+
+
+def dispatch_kernel(experts, quarter, picked, out, s1, r1, s2, r2, s3, r3, s4, r4):
     e, q, t = place(quarter)
-    lines, planes, partner = all_peers(experts, quarter, e, q, t)
-    greet(lines[1:] + planes[1:] + [partner])
+    lines = line_peers(experts, quarter, e, q, t)
+    sides, beside, below = plane_of(quarter, e, q, t)
+    partner = (e * quarter + q, 1 - t)
+    greet(lines[1:] + [beside, below, partner])
     sent = []
     hops = {}
     for k in range(1, experts):
@@ -131,35 +245,28 @@
         copy.start()
         sent.append(copy)
         hops[k] = copy
-    spread = {}
+    out[t, q, e] = picked[t, e]
     shared = []
-    for k in range(experts):
-        came = lax.rem(e - k + experts, experts)
-        if k == 0:
-            block = picked.at[t, e]
-            out[t, q, e] = picked[t, e]
-        else:
-            hops[k].wait_recv()
-            block = out.at[t, q, came]
-        for m in range(1, quarter):
-            copy = remote(block, out.at[t, q, came], s2.at[m, k], r2.at[m, k], planes[m])
-            copy.start()
-            sent.append(copy)
-            spread[m, k] = copy
-        copy = remote(block, out.at[t, q, came], s3.at[0, k], r3.at[0, k], partner)
+
+    def share(src, dst, i, k):
+        copy = remote(src, dst, s4.at[i, k], r4.at[i, k], partner)
         copy.start()
         sent.append(copy)
         shared.append(copy)
-    for k in range(experts):
-        came = lax.rem(e - k + experts, experts)
-        for m in range(1, quarter):
-            side = lax.rem(q - m + quarter, quarter)
-            spread[m, k].wait_recv()
-            block = out.at[t, side, came]
-            copy = remote(block, block, s3.at[m, k], r3.at[m, k], partner)
-            copy.start()
-            sent.append(copy)
-            shared.append(copy)
+
+    def block(k, came):
+        if k == 0:
+            src = picked.at[t, e]
+        else:
+            hops[k].wait_recv()
+            src = out.at[t, q, came]
+        share(src, out.at[t, q, came], 3, k)
+        return src
+
+    sent += gather_plane(
+        out, (t,), block, experts, e, q, sides, (beside, below),
+        lambda ref, i, k: share(ref, ref, i, k), s2, r2, s3, r3,
+    )
     for copy in shared:
         copy.wait_recv()
     for copy in sent:
@@ -167,8 +274,9 @@
 
 
 def dispatch(picked, quarter):
+    assert quarter == 4
     _, experts, capacity, width = picked.shape
-    sems = [(experts,), (experts,)] + [(quarter, experts)] * 4
+    sems = [(experts,)] * 2 + [(2, experts)] * 4 + [(4, experts)] * 2
     return pl.pallas_call(
         functools.partial(dispatch_kernel, experts, quarter),
         out_shape=jax.ShapeDtypeStruct((2, quarter, experts, capacity, width), picked.dtype),
@@ -180,57 +288,65 @@
 
 
 def collect_kernel(
-    experts, quarter, part, out, got0, sum0, got1, acc, low, s0, r0, s1, r1, s2, r2, s3, r3
+    experts, quarter, part, out, got0, sum0, low, s0, r0, s3, r3, s4, r4,
+    got, relay, got2, s1, r1, s2, r2,
 ):
     e, q, t = place(quarter)
-    lines, planes, partner = all_peers(experts, quarter, e, q, t)
-    greet(lines[1:] + planes[1:] + [partner])
+    lines = line_peers(experts, quarter, e, q, t)
+    sides, beside, below = plane_of(quarter, e, q, t)
+    partner = (e * quarter + q, 1 - t)
+    greet(lines[1:] + [beside, below, partner])
     sent = []
-    firsts = {}
-    order = list(range(1, quarter)) + [0]
-    for m in order:
-        side = lax.rem(q + m, quarter)
-        copy = remote(part.at[1 - t, side], got0.at[m], s0.at[m], r0.at[m], partner)
-        copy.start()
-        sent.append(copy)
-        firsts[m] = copy
-    seconds = {}
-    for m in order:
-        side = lax.rem(q + m, quarter)
-        firsts[m].wait_recv()
-        total = part[t, side].astype(jnp.float32) + got0[m].astype(jnp.float32)
-        if m == 0:
-            acc[...] = total
-        else:
-            sum0[m] = total.astype(jnp.bfloat16)
-            copy = remote(sum0.at[m], got1.at[m], s1.at[m], r1.at[m], planes[m])
+    halves = {}
+    places = (sides[2], sides[0], sides[1], q)
+    for k in list(range(1, experts)) + [0]:
+        ed = lax.rem(e + k, experts)
+        for m in range(quarter):
+            copy = remote(
+                part.at[1 - t, places[m], ed],
+                got0.at[places[m], ed],
+                s0.at[m, k],
+                r0.at[m, k],
+                partner,
+            )
             copy.start()
             sent.append(copy)
-            seconds[m] = copy
-    for m in range(1, quarter):
-        seconds[m].wait_recv()
-    total = acc[...]
-    for m in range(1, quarter):
-        total = total + got1[m].astype(jnp.float32)
-    low[...] = total.astype(jnp.bfloat16)
+            halves[m, k] = copy
+
+    def ready(k, ed):
+        for m in range(quarter):
+            halves[m, k].wait_recv()
+            sum0[places[m], ed] = (
+                part[t, places[m], ed].astype(jnp.float32)
+                + got0[places[m], ed].astype(jnp.float32)
+            ).astype(jnp.bfloat16)
+
     thirds = {}
-    for k in range(1, experts):
-        copy = remote(
-            low.at[lax.rem(e + k, experts)], out.at[t, e], s2.at[k], r2.at[k], lines[k]
-        )
-        copy.start()
-        sent.append(copy)
-        thirds[k] = copy
-    out[t, e] = low[e]
+    width = low.shape[-1]
+
+    def done(k, ed, totals):
+        for i in range(2):
+            low[k, :, i * width // 2 : (i + 1) * width // 2] = totals[i].astype(jnp.bfloat16)
+        if k > 0:
+            copy = remote(low.at[k], out.at[t, e], s3.at[k], r3.at[k], lines[k])
+            copy.start()
+            sent.append(copy)
+            thirds[k] = copy
+
+    sent += scatter_plane(
+        sum0, ready, done, experts, e, q, sides, (beside, below),
+        got, relay, got2, s1, r1, s2, r2,
+    )
+    out[t, e] = low[0]
     shared = []
     for k in range(experts):
         came = lax.rem(e - k + experts, experts)
         if k == 0:
-            block = low.at[e]
+            block = low.at[0]
         else:
             thirds[k].wait_recv()
             block = out.at[t, came]
-        copy = remote(block, out.at[t, came], s3.at[k], r3.at[k], partner)
+        copy = remote(block, out.at[t, came], s4.at[k], r4.at[k], partner)
         copy.start()
         sent.append(copy)
         shared.append(copy)
@@ -242,56 +358,66 @@
 
 def collect(part):
     _, quarter, experts, capacity, width = part.shape
+    assert quarter == 4
     low = part.dtype
-    block = (experts, capacity, width)
-    sems = [(quarter,)] * 4 + [(experts,)] * 4
+    block = (capacity, width)
+    sems = [(quarter, experts)] * 2 + [(experts,)] * 4
     return pl.pallas_call(
         functools.partial(collect_kernel, experts, quarter),
-        out_shape=jax.ShapeDtypeStruct((2, experts, capacity, width), low),
+        out_shape=jax.ShapeDtypeStruct((2, experts) + block, low),
         in_specs=in_vmem(1),
         out_specs=in_vmem(1)[0],
         scratch_shapes=[
-            pltpu.VMEM((quarter,) + block, low),
-            pltpu.VMEM((quarter,) + block, low),
-            pltpu.VMEM((quarter,) + block, low),
-            pltpu.VMEM(block, jnp.float32),
-            pltpu.VMEM(block, low),
+            pltpu.VMEM((quarter, experts) + block, low),
+            pltpu.VMEM((quarter, experts) + block, low),
+            pltpu.VMEM((experts,) + block, low),
         ]
-        + [pltpu.SemaphoreType.DMA(shape) for shape in sems],
+        + [pltpu.SemaphoreType.DMA(shape) for shape in sems]
+        + plane_scratch(experts, block, low),
         compiler_params=params(3),
     )(part)
 
 
 def reduce_kernel(
-    experts, quarter, g, small, out, small_out,
-    got1, sum1, got2, tiny1, mid, tiny2,
-    s1, r1, s2, r2, s3, r3, s4, r4, s5, r5, s6, r6,
+    experts, quarter, g, small, query_out, key_out, value_out, weight_out, small_out,
+    out, sum1, got3, tiny1, mid, tiny2,
+    s3, r3, s4, r4, s5, r5, s6, r6, s7, r7, s8, r8,
+    got, relay, got2, s1, r1, s2, r2,
 ):
     e, q, t = place(quarter)
-    lines, planes, _ = all_peers(experts, quarter, e, q, t)
-    greet(lines[1:] + planes[1:])
+    lines = line_peers(experts, quarter, e, q, t)
+    sides, beside, below = plane_of(quarter, e, q, t)
+    across = (e * quarter + sides[2], t)
+    planes = (beside, below, across)
+    greet(lines[1:] + [beside, below, across])
     sent = []
     tiny = []
-    for m in range(1, quarter):
+    for m in range(3):
         copy = remote(small, tiny1.at[q], s5.at[m], r5.at[m], planes[m])
         copy.start()
         sent.append(copy)
         tiny.append(copy)
     tiny1[q] = small[...]
-    order = list(range(1, experts)) + [0]
-    firsts = {}
-    for k in order:
-        for m in range(1, quarter):
-            copy = remote(
-                g.at[lax.rem(q + m, quarter), lax.rem(e + k, experts)],
-                got1.at[m, k],
-                s1.at[m, k],
-                r1.at[m, k],
-                planes[m],
-            )
+    width = out.shape[-1]
+    cols = [slice(i * width // 2, (i + 1) * width // 2) for i in range(2)]
+    seconds = {}
+    kept = []
+
+    def done(k, ed, totals):
+        if k > 0:
+            for i in range(2):
+                sum1[k, :, cols[i]] = totals[i].astype(jnp.bfloat16)
+            copy = remote(sum1.at[k], got3.at[k], s3.at[k], r3.at[k], lines[k])
             copy.start()
             sent.append(copy)
-            firsts[m, k] = copy
+            seconds[k] = copy
+        else:
+            kept.extend(totals)
+
+    sent += scatter_plane(
+        g, lambda k, ed: None, done, experts, e, q, sides, (beside, below),
+        got, relay, got2, s1, r1, s2, r2,
+    )
     for copy in tiny:
         copy.wait_recv()
     total = tiny1[0]
@@ -305,67 +431,74 @@
         copy.start()
         sent.append(copy)
         tiny.append(copy)
-    seconds = {}
-    for k in order:
-        total = g[q, lax.rem(e + k, experts)].astype(jnp.float32)
-        for m in range(1, quarter):
-            firsts[m, k].wait_recv()
-            total = total + got1[m, k].astype(jnp.float32)
-        if k > 0:
-            sum1[k] = total.astype(jnp.bfloat16)
-            copy = remote(sum1.at[k], got2.at[k], s2.at[k], r2.at[k], lines[k])
-            copy.start()
-            sent.append(copy)
-            seconds[k] = copy
     for k in range(1, experts):
         seconds[k].wait_recv()
-        total = total + got2[k].astype(jnp.float32)
-    sum1[0] = total.astype(jnp.bfloat16)
-    out[q, e] = total.astype(jnp.bfloat16)
+        for i in range(2):
+            kept[i] = kept[i] + got3[k, :, cols[i]].astype(jnp.float32)
+    for i in range(2):
+        sum1[0, :, cols[i]] = kept[i].astype(jnp.bfloat16)
+    out[q, e] = sum1[0]
     thirds = {}
     for k in range(1, experts):
-        copy = remote(sum1.at[0], out.at[q, e], s3.at[k], r3.at[k], lines[k])
+        copy = remote(sum1.at[0], out.at[q, e], s4.at[k], r4.at[k], lines[k])
         copy.start()
         sent.append(copy)
         thirds[k] = copy
-    last = []
-    for k in range(experts):
-        came = lax.rem(e - k + experts, experts)
+
+    def block(k, came):
         if k == 0:
-            block = sum1.at[0]
-        else:
-            thirds[k].wait_recv()
-            block = out.at[q, came]
-        for m in range(1, quarter):
-            copy = remote(block, out.at[q, came], s4.at[m, k], r4.at[m, k], planes[m])
-            copy.start()
-            sent.append(copy)
-            last.append(copy)
+            return sum1.at[0]
+        thirds[k].wait_recv()
+        return out.at[q, came]
+
+    sent += gather_plane(
+        out, (), block, experts, e, q, sides, (beside, below),
+        lambda ref, i, k: None, s7, r7, s8, r8,
+    )
     for copy in tiny:
         copy.wait_recv()
     total = tiny2[0]
     for k in range(1, experts):
         total = total + tiny2[k]
     small_out[...] = total
-    for copy in last:
-        copy.wait_recv()
     for copy in sent:
         copy.wait_send()
-
-
-def reduce_all(g, small):
+    piece = out.shape[2]
+    rows, half = query_out.shape
+    for number in range(quarter * experts):
+        at = number * piece
+        if at < rows:
+            whole = out[number // experts, number % experts].astype(jnp.float32)
+            query_out[at : at + piece] = whole[:, :half]
+            key_out[at : at + piece] = whole[:, half:]
+        elif at < rows + half:
+            at = at - rows
+            whole = out[number // experts, number % experts].astype(jnp.float32)
+            value_out[at : at + piece] = whole[:, :half]
+            value_out[half + at : half + at + piece] = whole[:, half:]
+        elif at < rows + 2 * half:
+            at = at - rows - half
+            whole = out[number // experts, number % experts].astype(jnp.float32)
+            weight_out[at : at + piece] = whole
+
+
+def reduce_all(g, small, rows, half):
     quarter, experts, piece, width = g.shape
+    assert quarter == 4 and width == 2 * half and rows == 2 * half and half % piece == 0
     low = g.dtype
-    both = (quarter, experts)
-    sems = [both, both] + [(experts,)] * 4 + [both, both] + [(quarter,)] * 2 + [(experts,)] * 2
+    sems = [(experts,)] * 4 + [(3,)] * 2 + [(experts,)] * 2 + [(2, experts)] * 4
+    tall = jax.ShapeDtypeStruct((rows, half), jnp.float32)
     return pl.pallas_call(
         functools.partial(reduce_kernel, experts, quarter),
         out_shape=(
-            jax.ShapeDtypeStruct(g.shape, low),
+            tall,
+            tall,
+            tall,
+            jax.ShapeDtypeStruct((half, width), jnp.float32),
             jax.ShapeDtypeStruct(small.shape, jnp.float32),
         ),
         in_specs=in_vmem(2),
-        out_specs=tuple(in_vmem(2)),
+        out_specs=tuple(in_vmem(5)),
         scratch_shapes=[
             pltpu.VMEM(g.shape, low),
             pltpu.VMEM((experts, piece, width), low),
@@ -374,7 +507,8 @@
             pltpu.VMEM(small.shape, jnp.float32),
             pltpu.VMEM((experts,) + small.shape, jnp.float32),
         ]
-        + [pltpu.SemaphoreType.DMA(shape) for shape in sems],
+        + [pltpu.SemaphoreType.DMA(shape) for shape in sems]
+        + plane_scratch(experts, (piece, width), low),
         compiler_params=params(4),
     )(g, small)
 
@@ -403,22 +537,27 @@
     return (amount + step - 1) // step * step
 
 
-def reduce_grads(large, small, experts, quarter):
-    width = large[0].shape[1]
-    stack = jnp.concatenate([one.astype(jnp.bfloat16) for one in large], axis=0)
-    rows = stack.shape[0]
-    piece = rows_up(-(-rows // (experts * quarter)), 16)
-    stack = jnp.pad(stack, ((0, piece * experts * quarter - rows), (0, 0)))
+def reduce_grads(query, key, value, weight, small, experts, quarter):
+    rows, half = query.shape
+    query, key, value, weight = [
+        one.astype(jnp.bfloat16) for one in (query, key, value, weight)
+    ]
+    stack = jnp.concatenate(
+        [
+            jnp.concatenate([query, key], axis=1),
+            jnp.concatenate([value[:half], value[half:]], axis=1),
+            weight,
+        ],
+        axis=0,
+    )
+    used, width = stack.shape
+    piece = rows_up(-(-used // (experts * quarter)), 16)
+    stack = jnp.pad(stack, ((0, piece * experts * quarter - used), (0, 0)))
     flat = jnp.concatenate([one.reshape(-1) for one in small])
     amount = flat.shape[0]
     flat = jnp.pad(flat, (0, rows_up(amount, 1024) - amount)).reshape(-1, 128)
-    done, tiny = reduce_all(stack.reshape(quarter, experts, piece, width), flat)
-    done = done.reshape(-1, width)
+    *wide, tiny = reduce_all(stack.reshape(quarter, experts, piece, width), flat, rows, half)
     tiny = tiny.reshape(-1)
-    wide, at = [], 0
-    for one in large:
-        wide.append(done[at : at + one.shape[0]].astype(jnp.float32))
-        at += one.shape[0]
     thin, at = [], 0
     for one in small:
         thin.append(tiny[at : at + one.size].reshape(one.shape))
@@ -609,10 +748,11 @@
     normed_grad = pair_sum(normed_part.astype(jnp.bfloat16), 1)
     input_part_grad, attn_gain_grad = rms_back(inputs, attn_gain, scale_one, normed_grad)
     tokens_grad = (middle_grad + input_part_grad).astype(jnp.bfloat16)
-    half = output_weight_grad.shape[0]
-    pieces = [output_weight_grad[:, at : at + half] for at in range(0, width, half)]
     wide, thin = reduce_grads(
-        [query_grad, key_grad, value_grad] + pieces,
+        query_grad,
+        key_grad,
+        value_grad,
+        output_weight_grad,
         [attn_gain_grad, table_grad, ffn_gain_grad, router_grad],
         experts,
         quarter,
@@ -622,7 +762,7 @@
         wide[0],
         wide[1],
         wide[2],
-        jnp.concatenate(wide[3:], axis=1),
+        wide[3],
         thin[1],
         thin[2],
         thin[3],

time: 158 us -> 171 us (1.082)
  local copies, waits for them, and re-layouts: 11 us -> 21.5 us
  other arithmetic: 10.8 us -> 14.1 us
    unnamed x43 -> x56, local copies, waits for them, and re-layouts: 3.85 us -> 12.2 us
    concatenate x1, other arithmetic: 1.09 us -> 7.14 us  [reduce_grads(): jnp.concatenate([jnp.concatenate([query, key], axis=1), jnp.concatenate([...]
    pallas_call x1, Pallas kernels: 27.4 us -> 22 us  [collect(): pl.pallas_call(functools.partial(collect_kernel, experts, quarter), out_s...]
    pallas_call x1, Pallas kernels: 58.8 us -> 62.9 us  [reduce_all(): pl.pallas_call(functools.partial(reduce_kernel, experts, quarter), out_sh...]
    convert_element_type x2 -> x0, other arithmetic: 2.82 us -> none  [reduce_grads(): wide.append(done[at:at + one.shape[0]].astype(jnp.float32))]
    concatenate x1, local copies, waits for them, and re-layouts: 0.05 us -> 2.44 us  [reduce_grads(): jnp.concatenate([jnp.concatenate([query, key], axis=1), jnp.concatenate([...]
where the time goes in v2:
time: 171 us; the launch traced here: 170 us
  Pallas kernels  113 us (66%)
  local copies, waits for them, and re-layouts  21.5 us (13%)
  matrix products  20.4 us (12%)
  other arithmetic  14.1 us (8%)
    pallas_call x1, Pallas kernels, reduce_all(): pl.pallas_call(functools.partial(reduce_kernel, experts, quarter), out_sh...  62.9 us
    pallas_call x1, Pallas kernels, dispatch(): pl.pallas_call(functools.partial(dispatch_kernel, experts, quarter), out_...  22.5 us
    pallas_call x1, Pallas kernels, collect(): pl.pallas_call(functools.partial(collect_kernel, experts, quarter), out_s...  22 us
    unnamed x56, local copies, waits for them, and re-layouts  12.2 us
    concatenate x1, other arithmetic, reduce_grads(): jnp.concatenate([jnp.concatenate([query, key], axis=1), jnp.concatenate([...  7.14 us
    slice x5, local copies, waits for them, and re-layouts, reduce_grads(): thin.append(tiny[at:at + one.size].reshape(one.shape))  3.79 us
    pallas_call x2, Pallas kernels, pair_sum(): pl.pallas_call(pair_kernel, out_shape=jax.ShapeDtypeStruct(x.shape, jnp.f...  3.45 us

profile of v2, /device:TPU:0, one launch (start us, length us, event | category | flops | bytes accessed | tf_op | source)
XLA Modules:
  0.0 169.9 jit_solution(18289247914147007955)
XLA Ops:
  0.7 0.8 compare_select_fusion
  1.5 0.7 fusion.49
  2.4 1.1 fusion.13
  3.4 0.9 fusion.10
  4.3 0.7 add_select_fusion
  5.0 0.9 convolution_bitcast_fusion.1
  5.9 0.7 pad.12.relative
  6.7 1.5 convolution_convert_fusion.9
  8.3 0.3 convolution_convert_fusion.8
  8.8 0.3 convolution_convert_fusion.10
  9.3 1.7 %shard_map.247 = f32[6,128,128]{2,1,0:T(8,128)} custom-call(f32[6,256]{1,0:T(8,128)} %pad.12.relative), custom_call_target="tpu_custom_call" | custom-call | tf_op jit(solution)/shard_map/pallas_call | solution.py:528
  11.0 1.4 fusion.63
  12.3 0.3 fusion.27
  12.7 0.4 convolution_convert_fusion.14
  13.1 0.3 copy-done.7
  13.4 0.3 fusion.66.x_ref
  13.7 1.9 %shard_map.248 = f32[128,768]{1,0:T(8,128)S(1)} custom-call(f32[128,768]{1,0:T(8,128)S(1)} %fusion.66.x_ref), custom_call_target="tpu_custom_call" | custom-call | tf_op jit(solution)/shard_map/pallas_call | solution.py:101
  16.3 0.3 convolution_convert_fusion
  16.8 22.5 %shard_map.249 = bf16[2,4,4,48,768]{4,3,2,1,0:T(8,128)(2,1)S(1)} custom-call(bf16[2,4,48,768]{3,2,1,0:T(8,128)(2,1)S(1)} %pad_maximum_fusion.2.picked), custom_call_target="tpu_custom_call" | custom-call | tf_op jit(solution)/shard_map/pallas_call | solution.py:280
  39.4 0.9 copy-done.16
  40.3 0.8 fusion.67
  41.1 1.4 fusion.7
  42.5 1.8 %fusion.69 = f32[768,384]{1,0:T(8,128)} fusion(bf16[768,768]{1,0:T(8,128)(2,1)S(1)} %bitcast.103, bf16[768,384]{1,0:T(8,128)(2,1)S(1)} %get-tuple-element.76), kind=kOutput, calls=%fused_computation.138 | convolution fusion | flops 452984832 | bytes 2949120 | tf_op jit(solution)/shard_map/rd,rf->df/dot_general | solution.py:701
  44.3 1.8 %fusion.52 = f32[384,768]{1,0:T(8,128)} fusion(bf16[768,768]{1,0:T(8,128)(2,1)S(1)} %bitcast.100, f32[768,384]{1,0:T(8,128)S(1)} %get-tuple-element.77), kind=kOutput, calls=%fused_computation.128 | convolution fusion | flops 455639040 | bytes 3538944 | tf_op jit(solution)/shard_map/rf,rd->fd/dot_general | solution.py:700
  46.1 0.9 convolution_convert_fusion.2
  47.1 0.8 convolution_convert_fusion.1
  48.1 22.0 %shard_map.250 = bf16[2,4,48,768]{3,2,1,0:T(8,128)(2,1)S(1)} custom-call(bf16[2,4,4,48,768]{4,3,2,1,0:T(8,128)(2,1)S(1)} %pad_maximum_fusion.part), custom_call_target="tpu_custom_call" | custom-call | tf_op jit(solution)/shard_map/pallas_call | solution.py:365
  70.1 0.3 convolution_bitcast_fusion
  70.4 0.8 fusion.12
  71.2 0.4 multiply_reduce_fusion
  71.8 0.3 convolution_convert_fusion.7
  72.2 0.3 convolution_convert_fusion.11
  73.0 0.4 multiply_reduce_fusion.1
  73.7 0.8 convolution_convert_fusion.12
  74.5 0.9 convolution_convert_fusion.13
  75.6 0.5 copy.77
  76.2 1.0 reshape.245
  77.7 0.5 copy-done.8
  78.3 0.3 fusion.68
  78.6 0.3 convolution_add_fusion.2
  78.9 0.4 copy-done.6
  79.4 0.3 fusion.8.x_ref
  79.7 1.6 shard_map.251
  81.6 0.9 fusion.19
  82.4 0.4 convolution_convert_fusion.6
  82.9 0.4 convolution_convert_fusion.3
  83.3 0.4 copy-done.15
  83.7 0.4 convolution_convert_fusion.4
  84.1 0.4 convolution_convert_fusion.5
  84.5 7.1 %pad_maximum_fusion.1 = bf16[1536,768]{0,1:T(8,128)(2,1)S(1)} fusion(bf16[384,768]{0,1:T(8,128)(2,1)S(1)} %convolution_convert_fusion.6, bf16[384,384]{0,1:T(8,128)(2,1)S(1)} %get-tuple-element.61, bf16[384,384]{0,1:T(8,128)(2,1)S(1)} %get-tuple-element.60, bf16[768,384]{0,1:T(8,128)(2,1)S(1)} %convolution_convert_fusion.4, ...), kind=kLoop, calls=%fused_computation.2 | loop fusion | flops 11796480 | bytes 4718592 | tf_op jit(solution)/shard_map/concatenate | solution.py:545
  91.7 2.4 %copy.66 = bf16[1536,768]{1,0:T(8,128)(2,1)} copy(bf16[1536,768]{0,1:T(8,128)(2,1)S(1)} %pad_maximum_fusion.1) | data formatting | bytes 4718592 | tf_op jit(solution)/shard_map/concatenate | solution.py:545
  94.1 62.9 %shard_map.252 = (f32[768,384]{1,0:T(8,128)S(1)}, f32[768,384]{1,0:T(8,128)S(1)}, f32[768,384]{1,0:T(8,128)S(1)}, f32[384,768]{1,0:T(8,128)S(1)}, f32[40,128]{1,0:T(8,128)S(1)}) custom-call(bf16[4,4,96,768]{3,2,1,0:T(8,128)(2,1)} %bitcast.97, f32[40,128]{1,0:T(8,128)S(1)} %pad_bitcast_fusion.1.small), custom_call_target="tpu_custom_call" | custom-call | tf_op jit(solution)/shard_map/pallas_call | solution.py:491
  157.1 1.0 copy-done.1
  158.1 1.0 copy-done.3
  159.1 0.7 slice.70
  159.7 0.6 slice_bitcast_fusion.2
  160.4 0.7 copy.69
  161.1 1.5 slice.60
  162.6 1.0 slice.71
  163.6 0.8 copy.70
  164.4 2.5 %copy.82 = f32[768,384]{1,0:T(8,128)} copy(f32[768,384]{1,0:T(8,128)} %copy-done.3) | data formatting | bytes 2359296
  166.9 1.0 copy.83
  167.9 1.0 copy.84
  168.9 1.0 copy.85
  (81 shorter events, 4.2 us)
Async XLA Ops:
  0.6 40.5 %copy-start = (bf16[768,384]{1,0:T(8,128)(2,1)S(1)}, bf16[768,384]{1,0:T(8,128)(2,1)}, u32[]{:S(2)}) copy-start(bf16[768,384]{1,0:T(8,128)(2,1)} %param.30) | copy-start | bytes 1769476
  0.7 7.7 %copy-start.4 = (bf16[128,768]{1,0:T(8,128)(2,1)S(1)}, bf16[128,768]{1,0:T(8,128)(2,1)}, u32[]{:S(2)}) copy-start(bf16[128,768]{1,0:T(8,128)(2,1)} %param.16) | copy-start | bytes 589828
  0.7 7.7 %copy-start.19 = (f32[768]{0:T(1024)S(1)}, f32[768]{0:T(1024)}, u32[]{:S(2)}) copy-start(f32[768]{0:T(1024)} %param.22) | copy-start | bytes 9220
  0.7 7.6 %copy-start.9 = (bf16[768,384]{1,0:T(8,128)(2,1)S(1)}, bf16[768,384]{1,0:T(8,128)(2,1)}, u32[]{:S(2)}) copy-start(bf16[768,384]{1,0:T(8,128)(2,1)} %param.24) | copy-start | bytes 1769476
  3.4 5.4 %copy-start.5 = (bf16[768,384]{1,0:T(8,128)(2,1)S(1)}, bf16[768,384]{1,0:T(8,128)(2,1)}, u32[]{:S(2)}) copy-start(bf16[768,384]{1,0:T(8,128)(2,1)} %param.25) | copy-start | bytes 1769476
  12.3 1.1 copy-start.7
  13.1 2.7 %copy-start.17 = (bf16[6,64,128]{2,1,0:T(8,128)(2,1)}, bf16[6,64,128]{2,1,0:T(8,128)(2,1)S(1)}, u32[]{:S(2)}) copy-start(bf16[6,64,128]{2,1,0:T(8,128)(2,1)S(1)} %convolution_convert_fusion.14) | copy-start | bytes 294916
  13.4 2.4 %copy-start.20 = (f32[768]{0:T(1024)S(1)}, f32[768]{0:T(1024)}, u32[]{:S(2)}) copy-start(f32[768]{0:T(1024)} %param.28) | copy-start | bytes 9220
  13.7 2.3 %copy-start.21 = (bf16[768,4]{0,1:T(4,128)(2,1)S(1)}, bf16[768,4]{0,1:T(4,128)(2,1)}, u32[]{:S(2)}) copy-start(bf16[768,4]{0,1:T(4,128)(2,1)} %param.29) | copy-start | bytes 18436
  13.7 2.5 %copy-start.22 = (s32[128,1]{0,1:T(1,128)S(1)}, s32[128,1]{0,1:T(1,128)}, u32[]{:S(2)}) copy-start(s32[128,1]{0,1:T(1,128)} %param.20) | copy-start | bytes 1540
  13.7 2.5 %copy-start.11 = (bf16[128,768]{1,0:T(8,128)(2,1)S(1)}, bf16[128,768]{1,0:T(8,128)(2,1)}, u32[]{:S(2)}) copy-start(bf16[128,768]{1,0:T(8,128)(2,1)} %param.17) | copy-start | bytes 589828
  39.3 1.1 copy-start.16
  76.2 1.1 copy-start.23
  76.2 1.5 copy-start.12
  77.2 1.1 copy-start.8
  77.2 1.4 copy-start.14
  77.3 1.3 copy-start.10
  78.2 1.1 copy-start.6
  79.7 2.7 %copy-start.18 = (bf16[6,64,128]{2,1,0:T(8,128)(2,1)S(1)}, bf16[6,64,128]{2,1,0:T(8,128)(2,1)}, u32[]{:S(2)}) copy-start(bf16[6,64,128]{2,1,0:T(8,128)(2,1)} %copy-done.17) | copy-start | bytes 294916
  82.8 0.9 copy-start.15
  83.2 0.9 copy-start.13
  157.0 1.0 copy-start.1
  158.1 1.0 copy-start.3
  164.4 2.5 %copy-start.2 = (f32[768,384]{1,0:T(8,128)S(1)}, f32[768,384]{1,0:T(8,128)}, u32[]{:S(2)}) copy-start(f32[768,384]{1,0:T(8,128)} %copy-done.1) | copy-start | bytes 3538948
